TPU v7x, 128 devices: a whole 4x4x4 slice. The times are simulated.
128 devices in a mesh: slab: 32 (over y, z, core), brick: 4 (over x).
Axes of the slice: x: 4, y: 4, z: 4, core: 2. Of those that a mesh axis runs over, the one named last changes fastest.
Arguments:
- charges: float32 [4, 131072], P(None, ('slab', 'brick')), may hold values from -8 to 8
- fractions: float32 [3, 131072], P(None, ('slab', 'brick')), may hold values from 0 to 1
- inner_cell: int32 [131072], P(('slab', 'brick')), may hold values from 0 to 4095
- dest_slab: int32 [131072, 1], P(('slab', 'brick')), may hold values from 0 to 31; in each aligned block of 1024 rows (0 to 1023, 1024 to 2047, ...) at most 64 rows name the same one
- filter_amp: float32 [2, 16], replicated, may hold values from -24 to 24
Outputs:
- potentials: float32 [4, 131072], P(None, ('slab', 'brick'))
Inputs may be any that keep to these rules, and one draw needn't show every extreme that they name: `dest_slab`: among the atoms of one device, no z-slab is named by more than 64 atoms.
All inputs are finite; a program needn't handle non-finite values.
Results may differ from a plain program's by a relative error of at most 0.0044.
Values may be sent and summed in bfloat16 or wider, within the bound.
A program may use at most 128 MiB of HBM per device.

v0:
```python
import math

import jax
import jax.numpy as jnp
from jax import lax
from jax.sharding import PartitionSpec as P

G = 256
BIN = 16


def from_partner(block, axis, distance):
    count = lax.axis_size(axis)
    route = []
    for low in range(count):
        high = low | 1 << distance
        if high != low and high < count:
            route += [(low, high), (high, low)]
    return lax.ppermute(block, axis, route)


def with_halo(cells, sides, width):
    for axis, dim in sides:
        count = lax.axis_size(axis)
        head = lax.slice_in_dim(cells, 0, width, axis=dim)
        tail = lax.slice_in_dim(cells, cells.shape[dim] - width, cells.shape[dim], axis=dim)
        cells = jnp.concatenate(
            [
                lax.ppermute(tail, axis, [(i, (i + 1) % count) for i in range(count)]),
                cells,
                lax.ppermute(head, axis, [((i + 1) % count, i) for i in range(count)]),
            ],
            axis=dim,
        )
    return cells


def spline_weights(fraction):
    remainder = 1.0 - fraction
    square = fraction * fraction
    cubed = square * fraction
    return (
        remainder * remainder * remainder / 6.0,
        (3.0 * cubed - 6.0 * square + 4.0) / 6.0,
        (-3.0 * cubed + 3.0 * square + 3.0 * fraction + 1.0) / 6.0,
        cubed / 6.0,
    )


def bump(magnitude, center, width):
    scaled = (magnitude - center * width) / width
    return jnp.exp(-0.5 * scaled * scaled)


def signed_freq(frequency, length):
    return jnp.where(frequency < length // 2, frequency, frequency - length).astype(jnp.float32)


def stencil(base_cell, fraction, length, start):
    weights = spline_weights(fraction)
    places = jnp.arange(length, dtype=jnp.int32)[None, :]
    running = jnp.zeros((base_cell.shape[0], length), jnp.float32)
    for offset in range(4):
        target = base_cell + start + offset
        running = running + jnp.where(places == target[:, None], weights[offset][:, None], 0.0)
    return running


def radial_gain(freq_z, freq_y, freq_x, filter_amp, length):
    along_z = signed_freq(freq_z, length)
    along_y = signed_freq(freq_y, length)
    along_x = signed_freq(freq_x, length)
    squares = (
        along_z[:, None, None] * along_z[:, None, None]
        + along_y[None, :, None] * along_y[None, :, None]
    )
    squares = squares + along_x[None, None, :] * along_x[None, None, :]
    magnitude = jnp.sqrt(squares)
    basis = jnp.stack(
        [bump(magnitude, float(center), float(BIN)) for center in range(filter_amp.shape[1])]
    )
    gains = jnp.dot(filter_amp, basis.reshape(basis.shape[0], -1), precision=lax.Precision.HIGHEST)
    return gains.reshape((filter_amp.shape[0],) + magnitude.shape)


def dft_tables(length):
    positions = jnp.arange(length, dtype=jnp.int32)
    phases = positions[:, None] * positions[None, :] % length
    angles = phases.astype(jnp.float32) * (2.0 * math.pi / length)
    return (jnp.cos(angles), jnp.sin(angles))


def along_axis(values, matrix_table, axis_pos):
    contracted = jnp.tensordot(
        values, matrix_table, axes=([axis_pos], [0]), precision=lax.Precision.HIGHEST
    )
    return jnp.moveaxis(contracted, -1, axis_pos)


def transform(real_part, imag_part, axis_pos, inverse):
    length = real_part.shape[axis_pos]
    cosine, sine_part = dft_tables(length)
    real_cos = along_axis(real_part, cosine, axis_pos)
    real_sin = along_axis(real_part, sine_part, axis_pos)
    imag_cos = along_axis(imag_part, cosine, axis_pos)
    imag_sin = along_axis(imag_part, sine_part, axis_pos)
    if inverse:
        factor_scale = 1.0 / length
        return ((real_cos - imag_sin) * factor_scale, (imag_cos + real_sin) * factor_scale)
    return (real_cos + imag_sin, imag_cos - real_sin)


def pair_swap(real_part, imag_part, bit_number):
    return from_partner((real_part, imag_part), ("slab", "brick"), bit_number)


def twiddle(device_id, block_size, section_level, axis_pos, array_rank):
    half_span = block_size * (1 << section_level)
    places = device_id * block_size + jnp.arange(block_size, dtype=jnp.int32)
    angles = (places % half_span).astype(jnp.float32) * (math.pi / half_span)
    view_shape = [1] * array_rank
    view_shape[axis_pos] = block_size
    is_upper = device_id // (1 << section_level) % 2 == 1
    return (jnp.cos(angles).reshape(view_shape), jnp.sin(angles).reshape(view_shape), is_upper)


def forward_section(real_part, imag_part, axis_pos, device_id, section_level, bit_number):
    cosine, sine_part, is_upper = twiddle(
        device_id, real_part.shape[axis_pos], section_level, axis_pos, real_part.ndim
    )
    other_real, other_imag = pair_swap(real_part, imag_part, bit_number)
    diff_real = other_real - real_part
    diff_imag = other_imag - imag_part
    new_real = jnp.where(
        is_upper, diff_real * cosine + diff_imag * sine_part, real_part + other_real
    )
    new_imag = jnp.where(
        is_upper, diff_imag * cosine - diff_real * sine_part, imag_part + other_imag
    )
    return (new_real, new_imag)


def inverse_section(real_part, imag_part, axis_pos, device_id, section_level, bit_number):
    cosine, sine_part, is_upper = twiddle(
        device_id, real_part.shape[axis_pos], section_level, axis_pos, real_part.ndim
    )
    send_real = jnp.where(is_upper, real_part * cosine - imag_part * sine_part, real_part)
    send_imag = jnp.where(is_upper, imag_part * cosine + real_part * sine_part, imag_part)
    other_real, other_imag = pair_swap(send_real, send_imag, bit_number)
    new_real = jnp.where(is_upper, other_real - send_real, send_real + other_real) * 0.5
    new_imag = jnp.where(is_upper, other_imag - send_imag, send_imag + other_imag) * 0.5
    return (new_real, new_imag)


def reversed_index(device_id, levels):
    result = jnp.zeros((), jnp.int32)
    for section_level in range(levels):
        result = result + device_id // (1 << section_level) % 2 * (1 << levels - 1 - section_level)
    return result


def fold_rim(extended, inner_size, axis_pos):
    core_part = lax.slice_in_dim(extended, 4, 4 + inner_size, axis=axis_pos)
    low_rim = lax.slice_in_dim(extended, 0, 2, axis=axis_pos)
    high_rim = lax.slice_in_dim(extended, inner_size + 6, inner_size + 8, axis=axis_pos)
    low_pad = [(0, 0)] * extended.ndim
    high_pad = [(0, 0)] * extended.ndim
    low_pad[axis_pos] = (0, inner_size - 2)
    high_pad[axis_pos] = (inner_size - 2, 0)
    return core_part + jnp.pad(low_rim, low_pad) + jnp.pad(high_rim, high_pad)


def body(charges, fractions, inner_cell, dest_slab, filter_amp):
    slab_count = lax.axis_size("slab")
    brick_count = lax.axis_size("brick")
    channels, local_atoms = charges.shape
    pair_count = channels // 2
    length = G
    slab_depth = length // slab_count
    height = length // brick_count
    capacity = 2 * local_atoms // slab_count
    slot_count = slab_count * capacity
    window = slab_depth + 4
    slab_index = lax.axis_index("slab")
    brick_index = lax.axis_index("brick")
    target = dest_slab[:, 0]
    z_local = inner_cell % slab_depth
    x_local = inner_cell // slab_depth % slab_depth
    y_local = inner_cell // (slab_depth * slab_depth)
    cell_codes = (z_local * height + y_local) * length + slab_index * slab_depth + x_local
    choose = (target[:, None] == jnp.arange(slab_count, dtype=jnp.int32)[None, :]).astype(jnp.int32)
    within = jnp.sum((jnp.cumsum(choose, axis=0) - 1) * choose, axis=1)
    payload = jnp.concatenate([charges, fractions], axis=0)
    outbound = (
        jnp.zeros((channels + 3, slab_count, capacity), jnp.float32)
        .at[:, target, within]
        .set(payload)
    )
    outcodes = (
        jnp.zeros((1, slab_count, capacity), jnp.int32)
        .at[:, target, within]
        .set(cell_codes[None, :])
    )
    inbound, incodes = (
        lax.all_to_all(outbound, "slab", split_axis=1, concat_axis=1, tiled=True),
        lax.all_to_all(outcodes, "slab", split_axis=1, concat_axis=1, tiled=True),
    )
    slot_charge = inbound[:channels].reshape(channels, slot_count)
    slot_frac = inbound[channels:].reshape(3, slot_count)
    slot_code = incodes.reshape(slot_count)
    slot_source = jnp.arange(slot_count, dtype=jnp.int32) // capacity
    slot_z = slot_code // (height * length)
    slot_y = slot_code // length % height
    slot_x = slot_code % length - slot_source * slab_depth
    weight_z = stencil(slot_z, slot_frac[0], slab_depth + 4, 1)
    weight_y = stencil(slot_y, slot_frac[1], height + 4, 1)
    weight_x = stencil(slot_x, slot_frac[2], window, 1)
    plane_weight = (
        (weight_z[:, :, None] * weight_y[:, None, :]).reshape(slot_count, -1).astype(jnp.bfloat16)
    )
    plane_rows = plane_weight.shape[1]
    plane_blocks = plane_weight.reshape(slab_count, capacity, plane_rows)
    line_blocks = weight_x.reshape(slab_count, capacity, window)
    charge_blocks = slot_charge.T.reshape(slab_count, capacity, channels)
    values = (charge_blocks[:, :, :, None] * line_blocks[:, :, None, :]).reshape(
        slab_count, capacity, channels * window
    )
    values = values.astype(jnp.bfloat16)
    tiles = lax.dot_general(
        plane_blocks, values, (((1,), (1,)), ((0,), (0,))), preferred_element_type=jnp.float32
    )
    tiles = tiles.reshape(slab_count, plane_rows, channels, window)
    core_part = tiles[:, :, :, 2 : slab_depth + 2]
    low_part = jnp.pad(tiles[:, :, :, 0:2], ((0, 0), (0, 0), (0, 0), (slab_depth - 2, 0)))
    high_part = jnp.pad(
        tiles[:, :, :, slab_depth + 2 : slab_depth + 4],
        ((0, 0), (0, 0), (0, 0), (0, slab_depth - 2)),
    )
    summed = core_part + jnp.roll(low_part, -1, axis=0) + jnp.roll(high_part, 1, axis=0)
    spread_mesh = jnp.transpose(summed, (1, 2, 0, 3)).reshape(
        slab_depth + 4, height + 4, channels, length
    )
    extended = with_halo(spread_mesh, (("slab", 0), ("brick", 1)), 2)
    density = fold_rim(fold_rim(extended, slab_depth, 0), height, 1)
    field = jnp.transpose(density, (2, 0, 1, 3))
    real_part = field[:pair_count]
    imag_part = field[pair_count:]
    real_part, imag_part = transform(real_part, imag_part, 3, False)
    slab_levels = slab_count.bit_length() - 1
    brick_levels = brick_count.bit_length() - 1
    for section_level in reversed(range(brick_levels)):
        real_part, imag_part = forward_section(
            real_part, imag_part, 2, brick_index, section_level, section_level
        )
    real_part, imag_part = transform(real_part, imag_part, 2, False)
    for section_level in reversed(range(slab_levels)):
        real_part, imag_part = forward_section(
            real_part, imag_part, 1, slab_index, section_level, brick_levels + section_level
        )
    real_part, imag_part = transform(real_part, imag_part, 1, False)
    freq_z = jnp.arange(slab_depth, dtype=jnp.int32) * slab_count + reversed_index(
        slab_index, slab_levels
    )
    freq_y = jnp.arange(height, dtype=jnp.int32) * brick_count + reversed_index(
        brick_index, brick_levels
    )
    gains = radial_gain(freq_z, freq_y, jnp.arange(length, dtype=jnp.int32), filter_amp, length)
    real_part = real_part * gains
    imag_part = imag_part * gains
    real_part, imag_part = transform(real_part, imag_part, 1, True)
    for section_level in range(slab_levels):
        real_part, imag_part = inverse_section(
            real_part, imag_part, 1, slab_index, section_level, brick_levels + section_level
        )
    real_part, imag_part = transform(real_part, imag_part, 2, True)
    for section_level in range(brick_levels):
        real_part, imag_part = inverse_section(
            real_part, imag_part, 2, brick_index, section_level, section_level
        )
    real_part, imag_part = transform(real_part, imag_part, 3, True)
    potential = jnp.concatenate([real_part, imag_part], axis=0)
    potential = jnp.transpose(potential, (1, 2, 0, 3)).astype(jnp.bfloat16)
    padded = with_halo(potential, (("slab", 0), ("brick", 1)), 2)
    flat_field = padded.reshape(plane_rows, channels, length)
    window_cells = (
        jnp.arange(slab_count, dtype=jnp.int32)[:, None] * slab_depth
        - 2
        + jnp.arange(window, dtype=jnp.int32)[None, :]
    ) % length
    windows = jnp.take(flat_field, window_cells.reshape(-1), axis=2)
    windows = windows.reshape(plane_rows, channels, slab_count, window)
    windows = jnp.transpose(windows, (2, 0, 1, 3)).reshape(
        slab_count, plane_rows, channels * window
    )
    mixed = lax.dot_general(
        plane_blocks, windows, (((2,), (1,)), ((0,), (0,))), preferred_element_type=jnp.float32
    )
    mixed = mixed.reshape(slab_count, capacity, channels, window)
    readings = jnp.sum(mixed * line_blocks[:, :, None, :], axis=3)
    readings = jnp.transpose(readings, (2, 0, 1))
    returned = lax.all_to_all(readings, "slab", split_axis=1, concat_axis=1, tiled=True)
    return returned[:, target, within]


def solution(mesh):
    in_specs = (
        P(None, ("slab", "brick")),
        P(None, ("slab", "brick")),
        P(("slab", "brick")),
        P(("slab", "brick"), None),
        P(),
    )
    out_specs = P(None, ("slab", "brick"))
    return jax.shard_map(body, mesh=mesh, in_specs=in_specs, out_specs=out_specs, check_vma=False)
```

profile of v0, /device:TPU:0, one launch (start us, length us, event | category | flops | bytes accessed | tf_op | source)
XLA Modules:
  0.0 868.8 jit_solution(673382991058198778)
XLA Ops:
  130.9 22.0 %collective-permute-done.5 = f32[2,8,64,256]{3,2,1,0:T(8,128)S(1)} collective-permute-done((f32[2,8,64,256]{3,2,1,0:T(8,128)S(1)}, f32[2,8,64,256]{3,2,1,0:T(8,128)S(1)}, u32[]{:S(2)}, u32[]{:S(2)}) %collective-permute-start.5) | collective-permute-done | bytes 1048608 | tf_op jit(solution)/shard_map/ppermute | solution.py:19
  152.9 20.9 %collective-permute-done.4 = f32[2,8,64,256]{3,2,1,0:T(8,128)} collective-permute-done((f32[2,8,64,256]{3,2,1,0:T(8,128)S(1)}, f32[2,8,64,256]{3,2,1,0:T(8,128)}, u32[]{:S(2)}, u32[]{:S(2)}) %collective-permute-start.4) | collective-permute-done | bytes 1048608 | tf_op jit(solution)/shard_map/ppermute | solution.py:19
  179.4 23.6 %collective-permute-done.6 = f32[2,8,64,256]{3,2,1,0:T(8,128)S(1)} collective-permute-done((f32[2,8,64,256]{3,2,1,0:T(8,128)S(1)}, f32[2,8,64,256]{3,2,1,0:T(8,128)S(1)}, u32[]{:S(2)}, u32[]{:S(2)}) %collective-permute-start.6) | collective-permute-done | bytes 1048608 | tf_op jit(solution)/shard_map/ppermute | solution.py:19
  203.1 19.9 %collective-permute-done.7 = f32[2,8,64,256]{3,2,1,0:T(8,128)S(1)} collective-permute-done((f32[2,8,64,256]{3,2,1,0:T(8,128)}, f32[2,8,64,256]{3,2,1,0:T(8,128)S(1)}, u32[]{:S(2)}, u32[]{:S(2)}) %collective-permute-start.7) | collective-permute-done | bytes 1048608 | tf_op jit(solution)/shard_map/ppermute | solution.py:19
  233.2 22.8 %collective-permute-done.8 = f32[2,8,64,256]{3,2,1,0:T(8,128)S(1)} collective-permute-done((f32[2,8,64,256]{3,2,1,0:T(8,128)S(1)}, f32[2,8,64,256]{3,2,1,0:T(8,128)S(1)}, u32[]{:S(2)}, u32[]{:S(2)}) %collective-permute-start.8) | collective-permute-done | bytes 1048608 | tf_op jit(solution)/shard_map/ppermute | solution.py:19
  256.0 19.1 %collective-permute-done.9 = f32[2,8,64,256]{3,2,1,0:T(8,128)} collective-permute-done((f32[2,8,64,256]{3,2,1,0:T(8,128)S(1)}, f32[2,8,64,256]{3,2,1,0:T(8,128)}, u32[]{:S(2)}, u32[]{:S(2)}) %collective-permute-start.9) | collective-permute-done | bytes 1048608 | tf_op jit(solution)/shard_map/ppermute | solution.py:19
  280.4 24.2 %collective-permute-done.10 = f32[2,8,64,256]{3,2,1,0:T(8,128)S(1)} collective-permute-done((f32[2,8,64,256]{3,2,1,0:T(8,128)}, f32[2,8,64,256]{3,2,1,0:T(8,128)S(1)}, u32[]{:S(2)}, u32[]{:S(2)}) %collective-permute-start.10) | collective-permute-done | bytes 1048608 | tf_op jit(solution)/shard_map/ppermute | solution.py:19
  304.6 18.3 %collective-permute-done.11 = f32[2,8,64,256]{3,2,1,0:T(8,128)S(1)} collective-permute-done((f32[2,8,64,256]{3,2,1,0:T(8,128)S(1)}, f32[2,8,64,256]{3,2,1,0:T(8,128)S(1)}, u32[]{:S(2)}, u32[]{:S(2)}) %collective-permute-start.11) | collective-permute-done | bytes 1048608 | tf_op jit(solution)/shard_map/ppermute | solution.py:19
  330.0 24.0 %collective-permute-done.12 = f32[2,8,64,256]{3,2,1,0:T(8,128)S(1)} collective-permute-done((f32[2,8,64,256]{3,2,1,0:T(8,128)S(1)}, f32[2,8,64,256]{3,2,1,0:T(8,128)S(1)}, u32[]{:S(2)}, u32[]{:S(2)}) %collective-permute-start.12) | collective-permute-done | bytes 1048608 | tf_op jit(solution)/shard_map/ppermute | solution.py:19
  354.0 17.5 %collective-permute-done.13 = f32[2,8,64,256]{3,2,1,0:T(8,128)} collective-permute-done((f32[2,8,64,256]{3,2,1,0:T(8,128)S(1)}, f32[2,8,64,256]{3,2,1,0:T(8,128)}, u32[]{:S(2)}, u32[]{:S(2)}) %collective-permute-start.13) | collective-permute-done | bytes 1048608 | tf_op jit(solution)/shard_map/ppermute | solution.py:19
  381.8 23.8 %collective-permute-done.14 = f32[2,8,64,256]{3,2,1,0:T(8,128)S(1)} collective-permute-done((f32[2,8,64,256]{3,2,1,0:T(8,128)S(1)}, f32[2,8,64,256]{3,2,1,0:T(8,128)S(1)}, u32[]{:S(2)}, u32[]{:S(2)}) %collective-permute-start.14) | collective-permute-done | bytes 1048608 | tf_op jit(solution)/shard_map/ppermute | solution.py:19
  405.6 19.4 %collective-permute-done.15 = f32[2,8,64,256]{3,2,1,0:T(8,128)} collective-permute-done((f32[2,8,64,256]{3,2,1,0:T(8,128)S(1)}, f32[2,8,64,256]{3,2,1,0:T(8,128)}, u32[]{:S(2)}, u32[]{:S(2)}) %collective-permute-start.15) | collective-permute-done | bytes 1048608 | tf_op jit(solution)/shard_map/ppermute | solution.py:19
  465.1 23.7 %stack.2 = f32[16,131072]{1,0:T(8,128)} concatenate(f32[1,131072]{1,0:T(1,128)S(1)} %reshape.1637, f32[1,131072]{1,0:T(1,128)} %reshape.1653, f32[1,131072]{1,0:T(1,128)} %reshape.1654, f32[1,131072]{1,0:T(1,128)} %reshape.1655, f32[1,131072]{1,0:T(1,128)} %reshape.1656, f32[1,131072]{1,0:T(1,128)} %reshape.1657, f32[1,131072]{1,0:T(1,128)} %reshape.1658, ...), dimensions={0} | concatenate | bytes 16777216 | tf_op jit(solution)/shard_map/stack | solution.py:79
  519.3 23.9 %collective-permute-done.20 = f32[2,8,64,256]{3,2,1,0:T(8,128)S(1)} collective-permute-done((f32[2,8,64,256]{3,2,1,0:T(8,128)S(1)}, f32[2,8,64,256]{3,2,1,0:T(8,128)S(1)}, u32[]{:S(2)}, u32[]{:S(2)}) %collective-permute-start.20) | collective-permute-done | bytes 1048608 | tf_op jit(solution)/shard_map/ppermute | solution.py:19
  543.2 21.7 %collective-permute-done.21 = f32[2,8,64,256]{3,2,1,0:T(8,128)S(1)} collective-permute-done((f32[2,8,64,256]{3,2,1,0:T(8,128)S(1)}, f32[2,8,64,256]{3,2,1,0:T(8,128)S(1)}, u32[]{:S(2)}, u32[]{:S(2)}) %collective-permute-start.21) | collective-permute-done | bytes 1048608 | tf_op jit(solution)/shard_map/ppermute | solution.py:19
  569.4 23.9 %collective-permute-done.22 = f32[2,8,64,256]{3,2,1,0:T(8,128)S(1)} collective-permute-done((f32[2,8,64,256]{3,2,1,0:T(8,128)S(1)}, f32[2,8,64,256]{3,2,1,0:T(8,128)S(1)}, u32[]{:S(2)}, u32[]{:S(2)}) %collective-permute-start.22) | collective-permute-done | bytes 1048608 | tf_op jit(solution)/shard_map/ppermute | solution.py:19
  593.3 21.0 %collective-permute-done.23 = f32[2,8,64,256]{3,2,1,0:T(8,128)S(1)} collective-permute-done((f32[2,8,64,256]{3,2,1,0:T(8,128)S(1)}, f32[2,8,64,256]{3,2,1,0:T(8,128)S(1)}, u32[]{:S(2)}, u32[]{:S(2)}) %collective-permute-start.23) | collective-permute-done | bytes 1048608 | tf_op jit(solution)/shard_map/ppermute | solution.py:19
  617.2 24.0 %collective-permute-done.24 = f32[2,8,64,256]{3,2,1,0:T(8,128)S(1)} collective-permute-done((f32[2,8,64,256]{3,2,1,0:T(8,128)S(1)}, f32[2,8,64,256]{3,2,1,0:T(8,128)S(1)}, u32[]{:S(2)}, u32[]{:S(2)}) %collective-permute-start.24) | collective-permute-done | bytes 1048608 | tf_op jit(solution)/shard_map/ppermute | solution.py:19
  641.2 20.1 %collective-permute-done.25 = f32[2,8,64,256]{3,2,1,0:T(8,128)S(1)} collective-permute-done((f32[2,8,64,256]{3,2,1,0:T(8,128)S(1)}, f32[2,8,64,256]{3,2,1,0:T(8,128)S(1)}, u32[]{:S(2)}, u32[]{:S(2)}) %collective-permute-start.25) | collective-permute-done | bytes 1048608 | tf_op jit(solution)/shard_map/ppermute | solution.py:19
  665.7 24.0 %collective-permute-done.26 = f32[2,8,64,256]{3,2,1,0:T(8,128)S(1)} collective-permute-done((f32[2,8,64,256]{3,2,1,0:T(8,128)S(1)}, f32[2,8,64,256]{3,2,1,0:T(8,128)S(1)}, u32[]{:S(2)}, u32[]{:S(2)}) %collective-permute-start.26) | collective-permute-done | bytes 1048608 | tf_op jit(solution)/shard_map/ppermute | solution.py:19
  691.1 17.8 %collective-permute-done.27 = f32[2,8,64,256]{3,2,1,0:T(8,128)S(1)} collective-permute-done((f32[2,8,64,256]{3,2,1,0:T(8,128)S(1)}, f32[2,8,64,256]{3,2,1,0:T(8,128)S(1)}, u32[]{:S(2)}, u32[]{:S(2)}) %collective-permute-start.27) | collective-permute-done | bytes 1048608 | tf_op jit(solution)/shard_map/ppermute | solution.py:19
  715.6 24.0 %collective-permute-done.28 = f32[2,8,64,256]{3,2,1,0:T(8,128)S(1)} collective-permute-done((f32[2,8,64,256]{3,2,1,0:T(8,128)S(1)}, f32[2,8,64,256]{3,2,1,0:T(8,128)S(1)}, u32[]{:S(2)}, u32[]{:S(2)}) %collective-permute-start.28) | collective-permute-done | bytes 1048608 | tf_op jit(solution)/shard_map/ppermute | solution.py:19
  739.6 18.3 %collective-permute-done.29 = f32[2,8,64,256]{3,2,1,0:T(8,128)S(1)} collective-permute-done((f32[2,8,64,256]{3,2,1,0:T(8,128)S(1)}, f32[2,8,64,256]{3,2,1,0:T(8,128)S(1)}, u32[]{:S(2)}, u32[]{:S(2)}) %collective-permute-start.29) | collective-permute-done | bytes 1048608 | tf_op jit(solution)/shard_map/ppermute | solution.py:19
  762.5 23.7 %collective-permute-done.31 = f32[2,8,64,256]{3,2,1,0:T(8,128)S(1)} collective-permute-done((f32[2,8,64,256]{3,2,1,0:T(8,128)S(1)}, f32[2,8,64,256]{3,2,1,0:T(8,128)S(1)}, u32[]{:S(2)}, u32[]{:S(2)}) %collective-permute-start.31) | collective-permute-done | bytes 1048608 | tf_op jit(solution)/shard_map/ppermute | solution.py:19
  (265 shorter events, 345.7 us)
Async XLA Ops:
  125.2 27.7 %collective-permute-start.5 = (f32[2,8,64,256]{3,2,1,0:T(8,128)S(1)}, f32[2,8,64,256]{3,2,1,0:T(8,128)S(1)}, u32[]{:S(2)}, u32[]{:S(2)}) collective-permute-start(f32[2,8,64,256]{3,2,1,0:T(8,128)S(1)} %convolution_subtract_fusion), channel_id=1, source_target_pairs={{0,2},{2,0},{1,3},{3,1},{4,6},{6,4},{5,7},{7,5},{8,10},{10,8},{9,1... | collective-permute-start | bytes 3145736 | tf_op jit(solution)/shard_map/ppermute | solution.py:19
  130.0 43.8 %collective-permute-start.4 = (f32[2,8,64,256]{3,2,1,0:T(8,128)S(1)}, f32[2,8,64,256]{3,2,1,0:T(8,128)}, u32[]{:S(2)}, u32[]{:S(2)}) collective-permute-start(f32[2,8,64,256]{3,2,1,0:T(8,128)S(1)} %convolution_add_fusion), channel_id=1, source_target_pairs={{0,2},{2,0},{1,3},{3,1},{4,6},{6,4},{5,7},{7,5},{8,10},{10,8},{9,1... | collective-permute-start | bytes 3145736 | tf_op jit(solution)/shard_map/ppermute | solution.py:19
  178.3 44.6 %collective-permute-start.7 = (f32[2,8,64,256]{3,2,1,0:T(8,128)}, f32[2,8,64,256]{3,2,1,0:T(8,128)S(1)}, u32[]{:S(2)}, u32[]{:S(2)}) collective-permute-start(f32[2,8,64,256]{3,2,1,0:T(8,128)} %get-tuple-element.40), channel_id=1, source_target_pairs={{0,1},{1,0},{2,3},{3,2},{4,5},{5,4},{6,7},{7,6},{8,9},{9,8},{10,11... | collective-permute-start | bytes 3145736 | tf_op jit(solution)/shard_map/ppermute | solution.py:19
  228.3 27.7 %collective-permute-start.8 = (f32[2,8,64,256]{3,2,1,0:T(8,128)S(1)}, f32[2,8,64,256]{3,2,1,0:T(8,128)S(1)}, u32[]{:S(2)}, u32[]{:S(2)}) collective-permute-start(f32[2,8,64,256]{3,2,1,0:T(8,128)S(1)} %fusion.19), channel_id=1, source_target_pairs={{0,64},{64,0},{1,65},{65,1},{2,66},{66,2},{3,67},{67,3},{4,68},{68... | collective-permute-start | bytes 3145736 | tf_op jit(solution)/shard_map/ppermute | solution.py:19
  230.3 44.8 %collective-permute-start.9 = (f32[2,8,64,256]{3,2,1,0:T(8,128)S(1)}, f32[2,8,64,256]{3,2,1,0:T(8,128)}, u32[]{:S(2)}, u32[]{:S(2)}) collective-permute-start(f32[2,8,64,256]{3,2,1,0:T(8,128)S(1)} %fusion.18), channel_id=1, source_target_pairs={{0,64},{64,0},{1,65},{65,1},{2,66},{66,2},{3,67},{67,3},{4,68},{68... | collective-permute-start | bytes 3145736 | tf_op jit(solution)/shard_map/ppermute | solution.py:19
  278.3 26.3 %collective-permute-start.10 = (f32[2,8,64,256]{3,2,1,0:T(8,128)}, f32[2,8,64,256]{3,2,1,0:T(8,128)S(1)}, u32[]{:S(2)}, u32[]{:S(2)}) collective-permute-start(f32[2,8,64,256]{3,2,1,0:T(8,128)} %get-tuple-element.36), channel_id=1, source_target_pairs={{0,32},{32,0},{1,33},{33,1},{2,34},{34,2},{3,35},{35,3},{4,36},{36... | collective-permute-start | bytes 3145736 | tf_op jit(solution)/shard_map/ppermute | solution.py:19
  279.3 43.6 %collective-permute-start.11 = (f32[2,8,64,256]{3,2,1,0:T(8,128)S(1)}, f32[2,8,64,256]{3,2,1,0:T(8,128)S(1)}, u32[]{:S(2)}, u32[]{:S(2)}) collective-permute-start(f32[2,8,64,256]{3,2,1,0:T(8,128)S(1)} %get-tuple-element.35), channel_id=1, source_target_pairs={{0,32},{32,0},{1,33},{33,1},{2,34},{34,2},{3,35},{35,3},{4,36},{36... | collective-permute-start | bytes 3145736 | tf_op jit(solution)/shard_map/ppermute | solution.py:19
  326.4 27.7 %collective-permute-start.12 = (f32[2,8,64,256]{3,2,1,0:T(8,128)S(1)}, f32[2,8,64,256]{3,2,1,0:T(8,128)S(1)}, u32[]{:S(2)}, u32[]{:S(2)}) collective-permute-start(f32[2,8,64,256]{3,2,1,0:T(8,128)S(1)} %get-tuple-element.34), channel_id=1, source_target_pairs={{0,16},{16,0},{1,17},{17,1},{2,18},{18,2},{3,19},{19,3},{4,20},{20... | collective-permute-start | bytes 3145736 | tf_op jit(solution)/shard_map/ppermute | solution.py:19
  328.4 43.1 %collective-permute-start.13 = (f32[2,8,64,256]{3,2,1,0:T(8,128)S(1)}, f32[2,8,64,256]{3,2,1,0:T(8,128)}, u32[]{:S(2)}, u32[]{:S(2)}) collective-permute-start(f32[2,8,64,256]{3,2,1,0:T(8,128)S(1)} %get-tuple-element.33), channel_id=1, source_target_pairs={{0,16},{16,0},{1,17},{17,1},{2,18},{18,2},{3,19},{19,3},{4,20},{20... | collective-permute-start | bytes 3145736 | tf_op jit(solution)/shard_map/ppermute | solution.py:19
  374.0 31.6 %collective-permute-start.14 = (f32[2,8,64,256]{3,2,1,0:T(8,128)S(1)}, f32[2,8,64,256]{3,2,1,0:T(8,128)S(1)}, u32[]{:S(2)}, u32[]{:S(2)}) collective-permute-start(f32[2,8,64,256]{3,2,1,0:T(8,128)S(1)} %get-tuple-element.32), channel_id=1, source_target_pairs={{0,8},{8,0},{1,9},{9,1},{2,10},{10,2},{3,11},{11,3},{4,12},{12,4},... | collective-permute-start | bytes 3145736 | tf_op jit(solution)/shard_map/ppermute | solution.py:19
  381.5 43.5 %collective-permute-start.15 = (f32[2,8,64,256]{3,2,1,0:T(8,128)S(1)}, f32[2,8,64,256]{3,2,1,0:T(8,128)}, u32[]{:S(2)}, u32[]{:S(2)}) collective-permute-start(f32[2,8,64,256]{3,2,1,0:T(8,128)S(1)} %get-tuple-element.31), channel_id=1, source_target_pairs={{0,8},{8,0},{1,9},{9,1},{2,10},{10,2},{3,11},{11,3},{4,12},{12,4},... | collective-permute-start | bytes 3145736 | tf_op jit(solution)/shard_map/ppermute | solution.py:19
  428.3 68.0 %collective-permute-start.16 = (f32[2,8,64,256]{3,2,1,0:T(8,128)}, f32[2,8,64,256]{3,2,1,0:T(8,128)}, u32[]{:S(2)}, u32[]{:S(2)}) collective-permute-start(f32[2,8,64,256]{3,2,1,0:T(8,128)} %get-tuple-element.30), channel_id=1, source_target_pairs={{0,4},{4,0},{1,5},{5,1},{2,6},{6,2},{3,7},{7,3},{8,12},{12,8},{9,1... | collective-permute-start | bytes 3145736 | tf_op jit(solution)/shard_map/ppermute | solution.py:19
  428.3 68.0 %collective-permute-start.17 = (f32[2,8,64,256]{3,2,1,0:T(8,128)S(1)}, f32[2,8,64,256]{3,2,1,0:T(8,128)}, u32[]{:S(2)}, u32[]{:S(2)}) collective-permute-start(f32[2,8,64,256]{3,2,1,0:T(8,128)S(1)} %get-tuple-element.29), channel_id=1, source_target_pairs={{0,4},{4,0},{1,5},{5,1},{2,6},{6,2},{3,7},{7,3},{8,12},{12,8},{9,1... | collective-permute-start | bytes 3145736 | tf_op jit(solution)/shard_map/ppermute | solution.py:19
  518.9 45.9 %collective-permute-start.21 = (f32[2,8,64,256]{3,2,1,0:T(8,128)S(1)}, f32[2,8,64,256]{3,2,1,0:T(8,128)S(1)}, u32[]{:S(2)}, u32[]{:S(2)}) collective-permute-start(f32[2,8,64,256]{3,2,1,0:T(8,128)S(1)} %get-tuple-element.23), channel_id=1, source_target_pairs={{0,8},{8,0},{1,9},{9,1},{2,10},{10,2},{3,11},{11,3},{4,12},{12,4},... | collective-permute-start | bytes 3145736 | tf_op jit(solution)/shard_map/ppermute | solution.py:19
  565.6 27.7 %collective-permute-start.22 = (f32[2,8,64,256]{3,2,1,0:T(8,128)S(1)}, f32[2,8,64,256]{3,2,1,0:T(8,128)S(1)}, u32[]{:S(2)}, u32[]{:S(2)}) collective-permute-start(f32[2,8,64,256]{3,2,1,0:T(8,128)S(1)} %get-tuple-element.22), channel_id=1, source_target_pairs={{0,16},{16,0},{1,17},{17,1},{2,18},{18,2},{3,19},{19,3},{4,20},{20... | collective-permute-start | bytes 3145736 | tf_op jit(solution)/shard_map/ppermute | solution.py:19
  569.2 45.1 %collective-permute-start.23 = (f32[2,8,64,256]{3,2,1,0:T(8,128)S(1)}, f32[2,8,64,256]{3,2,1,0:T(8,128)S(1)}, u32[]{:S(2)}, u32[]{:S(2)}) collective-permute-start(f32[2,8,64,256]{3,2,1,0:T(8,128)S(1)} %get-tuple-element.21), channel_id=1, source_target_pairs={{0,16},{16,0},{1,17},{17,1},{2,18},{18,2},{3,19},{19,3},{4,20},{20... | collective-permute-start | bytes 3145736 | tf_op jit(solution)/shard_map/ppermute | solution.py:19
  615.0 26.2 %collective-permute-start.24 = (f32[2,8,64,256]{3,2,1,0:T(8,128)S(1)}, f32[2,8,64,256]{3,2,1,0:T(8,128)S(1)}, u32[]{:S(2)}, u32[]{:S(2)}) collective-permute-start(f32[2,8,64,256]{3,2,1,0:T(8,128)S(1)} %get-tuple-element.20), channel_id=1, source_target_pairs={{0,32},{32,0},{1,33},{33,1},{2,34},{34,2},{3,35},{35,3},{4,36},{36... | collective-permute-start | bytes 3145736 | tf_op jit(solution)/shard_map/ppermute | solution.py:19
  615.7 45.6 %collective-permute-start.25 = (f32[2,8,64,256]{3,2,1,0:T(8,128)S(1)}, f32[2,8,64,256]{3,2,1,0:T(8,128)S(1)}, u32[]{:S(2)}, u32[]{:S(2)}) collective-permute-start(f32[2,8,64,256]{3,2,1,0:T(8,128)S(1)} %get-tuple-element.19), channel_id=1, source_target_pairs={{0,32},{32,0},{1,33},{33,1},{2,34},{34,2},{3,35},{35,3},{4,36},{36... | collective-permute-start | bytes 3145736 | tf_op jit(solution)/shard_map/ppermute | solution.py:19
  662.0 27.7 %collective-permute-start.26 = (f32[2,8,64,256]{3,2,1,0:T(8,128)S(1)}, f32[2,8,64,256]{3,2,1,0:T(8,128)S(1)}, u32[]{:S(2)}, u32[]{:S(2)}) collective-permute-start(f32[2,8,64,256]{3,2,1,0:T(8,128)S(1)} %get-tuple-element.17), channel_id=1, source_target_pairs={{0,64},{64,0},{1,65},{65,1},{2,66},{66,2},{3,67},{67,3},{4,68},{68... | collective-permute-start | bytes 3145736 | tf_op jit(solution)/shard_map/ppermute | solution.py:19
  662.8 46.1 %collective-permute-start.27 = (f32[2,8,64,256]{3,2,1,0:T(8,128)S(1)}, f32[2,8,64,256]{3,2,1,0:T(8,128)S(1)}, u32[]{:S(2)}, u32[]{:S(2)}) collective-permute-start(f32[2,8,64,256]{3,2,1,0:T(8,128)S(1)} %get-tuple-element.18), channel_id=1, source_target_pairs={{0,64},{64,0},{1,65},{65,1},{2,66},{66,2},{3,67},{67,3},{4,68},{68... | collective-permute-start | bytes 3145736 | tf_op jit(solution)/shard_map/ppermute | solution.py:19
  713.4 26.2 %collective-permute-start.28 = (f32[2,8,64,256]{3,2,1,0:T(8,128)S(1)}, f32[2,8,64,256]{3,2,1,0:T(8,128)S(1)}, u32[]{:S(2)}, u32[]{:S(2)}) collective-permute-start(f32[2,8,64,256]{3,2,1,0:T(8,128)S(1)} %get-tuple-element.44), channel_id=1, source_target_pairs={{0,1},{1,0},{2,3},{3,2},{4,5},{5,4},{6,7},{7,6},{8,9},{9,8},{10,11... | collective-permute-start | bytes 3145736 | tf_op jit(solution)/shard_map/ppermute | solution.py:19
  715.0 42.9 %collective-permute-start.29 = (f32[2,8,64,256]{3,2,1,0:T(8,128)S(1)}, f32[2,8,64,256]{3,2,1,0:T(8,128)S(1)}, u32[]{:S(2)}, u32[]{:S(2)}) collective-permute-start(f32[2,8,64,256]{3,2,1,0:T(8,128)S(1)} %get-tuple-element.43), channel_id=1, source_target_pairs={{0,1},{1,0},{2,3},{3,2},{4,5},{5,4},{6,7},{7,6},{8,9},{9,8},{10,11... | collective-permute-start | bytes 3145736 | tf_op jit(solution)/shard_map/ppermute | solution.py:19
  758.5 27.7 %collective-permute-start.31 = (f32[2,8,64,256]{3,2,1,0:T(8,128)S(1)}, f32[2,8,64,256]{3,2,1,0:T(8,128)S(1)}, u32[]{:S(2)}, u32[]{:S(2)}) collective-permute-start(f32[2,8,64,256]{3,2,1,0:T(8,128)S(1)} %get-tuple-element.15), channel_id=1, source_target_pairs={{0,2},{2,0},{1,3},{3,1},{4,6},{6,4},{5,7},{7,5},{8,10},{10,8},{9,1... | collective-permute-start | bytes 3145736 | tf_op jit(solution)/shard_map/ppermute | solution.py:19
  762.0 43.2 %collective-permute-start.30 = (f32[2,8,64,256]{3,2,1,0:T(8,128)S(1)}, f32[2,8,64,256]{3,2,1,0:T(8,128)}, u32[]{:S(2)}, u32[]{:S(2)}) collective-permute-start(f32[2,8,64,256]{3,2,1,0:T(8,128)S(1)} %get-tuple-element.16), channel_id=1, source_target_pairs={{0,2},{2,0},{1,3},{3,1},{4,6},{6,4},{5,7},{7,5},{8,10},{10,8},{9,1... | collective-permute-start | bytes 3145736 | tf_op jit(solution)/shard_map/ppermute | solution.py:19
  (34 other events, 909.2 us)
where the time goes:
time: 878 us; the launch traced here: 869 us
  waiting for transfers between devices  535 us (61%)
  local copies, waits for them, and re-layouts  142 us (16%)
  starting transfers between devices  70.1 us (8%)
  other arithmetic  55.2 us (6%)
  matrix products  52.5 us (6%)
  blocking collectives  12.8 us (1%)
    ppermute x28, waiting for transfers between devices, from_partner(): return lax.ppermute(block, axis, route)  519 us
    ppermute x28, starting transfers between devices, from_partner(): return lax.ppermute(block, axis, route)  41.8 us
    dot_general x24, matrix products, along_axis(): jnp.tensordot(values, matrix_table, axes=([axis_pos], [0]), precision=lax...  41.1 us
    exp x16, local copies, waits for them, and re-layouts, bump(): return jnp.exp(-0.5 * scaled * scaled)  32.5 us
    another operation x1, local copies, waits for them, and re-layouts, radial_gain(): jnp.stack([bump(magnitude, float(center), float(BIN)) for center in range...  23.7 us
    convert_element_type x2, local copies, waits for them, and re-layouts, body(): (weight_z[:, :, None] * weight_y[:, None, :]).reshape(slot_count, -1)  18.1 us
  transfers between devices with their start and end apart: 38, of which 32 were waited for; matrix products, arithmetic and copies ran while one was open for 12% of the time, Pallas kernels for 0%

commit v1 on v0

v1 whole, which is shorter than its diff:
```python
import math

import numpy as np

import jax
import jax.numpy as jnp
import ml_dtypes
from jax import lax
from jax.experimental import pallas as pl
from jax.experimental.pallas import tpu as pltpu
from jax.sharding import PartitionSpec as P

G = 256
BIN = 16
SLABS = 32
BRICKS = 4
CAP = 64
BF = jnp.bfloat16
MESH = pl.DeviceIdType.MESH


def waves():
    places = np.arange(G)
    angles = 2.0 * np.pi * ((places[:, None] * places[None, :]) % G) / G
    return np.cos(angles), np.sin(angles)


def forward_table():
    cosine, sine = waves()
    return np.stack([np.stack([cosine, sine], 1), np.stack([-sine, cosine], 1)], 0)


def inverse_table():
    cosine, sine = waves()
    return np.stack([np.stack([cosine, -sine], 1), np.stack([sine, cosine], 1)], 0) / G


def spline_weights(fraction):
    remainder = 1.0 - fraction
    square = fraction * fraction
    cubed = square * fraction
    return (
        remainder * remainder * remainder / 6.0,
        (3.0 * cubed - 6.0 * square + 4.0) / 6.0,
        (-3.0 * cubed + 3.0 * square + 3.0 * fraction + 1.0) / 6.0,
        cubed / 6.0,
    )


GROUPS = 8
LANES = 256
PLACES = 132
WINDOW = 48
HALVES = 2
UNITS = 4
CHIP_ORDER = (
    (2, 2), (0, 1), (1, 0), (0, 3), (3, 0), (1, 2), (2, 1), (3, 2), (2, 3), (0, 2), (2, 0), (1, 1), (3, 3), (1, 3), (3, 1),
)
WIDE = 11
ROWS = 24
BACK_ROWS = 32
BACK_ORDER = (1, 2, 3, 4, 5, 6, 7, 8, 0, 9, 10)
VMEM_LIMIT = 56 * 1024 * 1024


def rounded_table(table):
    return np.ascontiguousarray(table).astype(ml_dtypes.bfloat16)


def rim_table():
    table = np.zeros((128, WIDE, 2, 64), np.float32)
    for x in range(WIDE):
        for r in range(2):
            for start, y in ((0, 0), (32, 1), (64, 63)):
                table[start + x * 2 + r, x, r, y] = 1.0
    return table.reshape(128, WIDE * 128)


def make_tables():
    forward = forward_table()
    inverse = inverse_table()
    both = np.stack(waves())
    where = np.arange(G)
    where = (where // 16 * 16 + where % 8 * 2 + where // 8 % 2 - 1) % G
    order = np.arange(G).reshape(SLABS, HALVES, 4).transpose(1, 0, 2).reshape(G)
    tables = (
        rim_table(),
        both[:, order][:, :, where].reshape(2, HALVES, 128, G).transpose(1, 0, 2, 3).reshape(512, G),
        both.reshape(512, G),
        forward.reshape(2, G, 2, BRICKS, 64).transpose(3, 2, 4, 0, 1).reshape(512, 512),
        inverse.reshape(2, BRICKS, 64, 2, G).transpose(3, 4, 1, 0, 2).reshape(512, 512),
        both.reshape(512, G) / G,
        both[:, where][:, :, order].reshape(512, G) / G,
    )
    return [rounded_table(table) for table in tables]


def dot(a, b):
    return lax.dot_general(a, b, (((1,), (0,)), ((), ())), preferred_element_type=jnp.float32)


def dot_nt(a, b):
    return lax.dot_general(a, b, (((1,), (1,)), ((), ())), preferred_element_type=jnp.float32)


def iota(shape, dim):
    return lax.broadcasted_iota(jnp.int32, shape, dim)


def double(values):
    high = values.astype(BF).astype(jnp.float32)
    return high, values - high


def dense(cell, fraction, places):
    weights = spline_weights(fraction)
    total = 0.0
    for j in range(4):
        total = total + jnp.where(places == cell + j, weights[j], 0.0)
    return total


def slot_lanes(g):
    return pl.ds(pl.multiple_of(g * LANES, LANES), LANES)


def line_weights(held, places):
    code = held[7:8, :].astype(jnp.int32)
    return dense((code >> 3) & 7, held[6:7, :], places)


def remote(src, dst, sems, at, target):
    copy = pltpu.make_async_remote_copy(
        src_ref=src,
        dst_ref=dst,
        send_sem=sems.at[0, at],
        recv_sem=sems.at[1, at],
        device_id=target,
        device_id_type=MESH,
    )
    copy.start()
    return copy


def kernel(
    charge_ref, frac_ref, cell_ref, target_ref, amp_ref,
    rim_far, zt_far, xt_far, yt_far, iyt_far, ixt_far, izt_far,
    out_ref,
    rim_ref, zt, xt, yt, iyt, ixt, izt,
    sorted_ref, read_ref, rank_ref, pairs, rim_pairs, rim_sums, rim_near, rim_part, mesh, mesh_back, slices,
    rim_out, rim_in, rim_out2, rim_in2, side_out, side_in, freq, freq_back,
    block, from_slab, to_brick, from_brick, back_brick, got_brick, back_slab, got_slab, after, potential, gain,
    table_sems, near_sems, slab_sems, brick_sems, brick_sems2, slab_sems2,
):
    slab = lax.axis_index("slab")
    brick = lax.axis_index("brick")
    left = {"slab": lax.rem(slab + SLABS - 1, SLABS)}
    right = {"slab": lax.rem(slab + 1, SLABS)}
    down = {"brick": lax.rem(brick + BRICKS - 1, BRICKS)}
    up = {"brick": lax.rem(brick + 1, BRICKS)}

    barrier = pltpu.get_barrier_semaphore()

    for step in range(1, SLABS):
        pl.semaphore_signal(
            barrier, inc=1, device_id={"slab": lax.rem(slab + step, SLABS)}, device_id_type=MESH
        )
    for step in range(1, BRICKS):
        pl.semaphore_signal(
            barrier, inc=1, device_id={"brick": lax.rem(brick + step, BRICKS)}, device_id_type=MESH
        )

    loads = []
    for at, (far, near) in enumerate(
        ((rim_far, rim_ref), (zt_far, zt), (xt_far, xt), (yt_far, yt), (iyt_far, iyt), (ixt_far, ixt), (izt_far, izt))
    ):
        load = pltpu.make_async_copy(far, near, table_sems.at[at])
        load.start()
        loads.append(load)

    atoms = charge_ref.shape[1]
    blocks = atoms // 128
    target = target_ref[...]
    here = jnp.where(iota((SLABS, atoms), 0) == target, 1.0, 0.0)
    stacked = jnp.concatenate([here[:, b * 128 : b * 128 + 128] for b in range(blocks)], axis=0).astype(BF)
    earlier = jnp.where(iota((128, 128), 0) < iota((128, 128), 1), 1.0, 0.0)
    counts = dot(stacked, jnp.concatenate([earlier, jnp.ones((128, 128), jnp.float32)], axis=1).astype(BF))
    ahead = jnp.zeros((SLABS, 128), jnp.float32)
    ranks = []
    for b in range(blocks):
        rows = slice(b * SLABS, b * SLABS + SLABS)
        ranks.append(counts[rows, 0:128] + ahead)
        ahead = ahead + counts[rows, 128:]
    rank = jnp.sum(here * jnp.concatenate(ranks, axis=1), axis=0, keepdims=True).astype(jnp.int32)
    rank_ref[...] = jnp.where((iota((128, atoms), 0) & 63) == rank, 1.0, 0.0).astype(BF)
    payload = jnp.concatenate([charge_ref[...], frac_ref[...], cell_ref[...].astype(jnp.float32)], axis=0)
    parts = double(payload)
    low_half = iota((8, 128), 1) < 64

    def sort(g, carry):
        rows = []
        for part in parts:
            rows += [jnp.where(target == g * 8 + t, part, 0.0) for t in range(8)]
        moved = dot_nt(jnp.concatenate(rows, axis=0).astype(BF), rank_ref[...])
        moved = moved[0:64] + moved[64:128]
        tiles = [
            jnp.where(low_half, moved[16 * t : 16 * t + 8], moved[16 * t + 8 : 16 * t + 16]) for t in range(4)
        ]
        sorted_ref[:, pl.ds(pl.multiple_of(g * 512, 512), 512)] = jnp.concatenate(tiles, axis=1)
        return carry

    lax.fori_loop(0, SLABS // 8, sort, 0, unroll=4)

    slab_of = iota((ROWS, LANES), 1) >> 6
    x_of = iota((ROWS, LANES), 0) >> 1
    first_part = (iota((ROWS, LANES), 0) & 1) == 0

    def line(held, p):
        return jnp.where(first_part, held[p : p + 1, :], held[2 + p : 3 + p, :]) * line_weights(held, x_of)

    rim_sums[...] = jnp.zeros(rim_sums.shape, jnp.float32)
    window_row = iota((WINDOW, LANES), 0)
    window_place = (window_row >> 4) * 16 + (window_row & 7) * 2 + ((window_row >> 3) & 1)
    slab_start = (iota((1, LANES), 1) >> 6) * 8

    def make_rims(g, carry):
        held = sorted_ref[:, slot_lanes(g)]
        code = held[7:8, :].astype(jnp.int32)
        wz = dense((code & 7) + slab_start, held[4:5, :], window_place)
        lines = [line(held, p) for p in range(2)]
        blocks, columns = [], []
        for h, y in enumerate((64, 65, -1)):
            rim = (wz * dense((code >> 6) - 1, held[5:6, :], y)).astype(BF)
            rim_pairs[g, pl.ds(h * WINDOW, WINDOW), :] = rim
            blocks.append(rim)
            rows = []
            for p in range(2):
                if h:
                    rows.append(jnp.zeros((32 * h, LANES), jnp.float32))
                rows += [lines[p], jnp.zeros((128 - ROWS - 32 * h, LANES), jnp.float32)]
            columns.append(jnp.concatenate(rows, axis=0).astype(BF))
        at = pl.ds(pl.multiple_of(g * 32, 16), WINDOW)
        rim_sums[at, :] = rim_sums[at, :] + dot_nt(
            jnp.concatenate(blocks, axis=1), jnp.concatenate(columns, axis=1)
        )
        return carry

    lax.fori_loop(0, GROUPS, make_rims, 0, unroll=4)
    rim_sums[0:16, :] = rim_sums[0:16, :] + rim_sums[G : G + 16, :]
    near = {}
    for p in range(2):
        rim_out[p] = rim_sums[0:G, p * 128 : p * 128 + 128].astype(BF)
    pl.semaphore_wait(barrier, SLABS - 1 + BRICKS - 1)
    for p in range(2):
        near["up", p] = remote(rim_out.at[p], rim_in.at[p, 0], near_sems, 8 * p, up)
        near["down", p] = remote(rim_out.at[p], rim_in.at[p, 1], near_sems, 8 * p + 1, down)

    mesh[:, 0:2] = jnp.zeros((2, 2, ROWS, 128), jnp.float32)

    def spread(p):
        def one(g, carry):
            held = sorted_ref[:, slot_lanes(g)]
            if p == 0:
                code = held[7:8, :].astype(jnp.int32)
                wz = dense(code & 7, held[4:5, :], iota((16, LANES), 0))
                wy = dense((code >> 6) - 1, held[5:6, :], iota((64, LANES), 0))
            own = line(held, p)
            lines = jnp.concatenate([jnp.where(slab_of == i, own, 0.0) for i in range(4)], axis=0).astype(BF)
            for z in (4, 8, 0):
                if p == 0:
                    pairs[g, z // 4] = jnp.concatenate(
                        [wy * wz[z + k : z + k + 1, :] for k in range(4)], axis=0
                    ).astype(BF)
                tile = dot_nt(lines, pairs[g, z // 4])
                for i in range(4):
                    for side in range(2):
                        at = g * 16 + i * 4 + z // 2 + side
                        part = tile[i * ROWS : i * ROWS + ROWS, side * 128 : side * 128 + 128]
                        mesh[p, at] = part if z else mesh[p, at] + part
            return carry

        lax.fori_loop(0, GROUPS, one, 0, unroll=4)
        mesh[p, 0] = mesh[p, 0] + mesh[p, 128]
        mesh[p, 1] = mesh[p, 1] + mesh[p, 129]

    low_all = iota((G, 128), 1) < 64
    sign = jnp.where(low_all, 1.0, -1.0)

    def turn(values):
        return sign[0 : values.shape[0]] * pltpu.roll(values, 64, 1)

    def cut(p):
        def one(step, carry):
            for part in range(3):
                turned = jnp.swapaxes(mesh[p, pl.ds(step * 8, 8), pl.ds(part * 8, 8), :], 0, 1)
                for x in range(4 * part, min(4 * part + 4, WIDE)):
                    a, b = turned[x % 4 * 2], turned[x % 4 * 2 + 1]
                    slices[p, x, pl.ds(pl.multiple_of(step * 16, 16), 16), :] = jnp.concatenate(
                        [
                            jnp.where(low_half, a, pltpu.roll(b, 64, 1)),
                            jnp.where(low_half, pltpu.roll(a, 64, 1), b),
                        ],
                        axis=0,
                    )
            return carry

        lax.fori_loop(0, 16, one, 0, unroll=2)

    def pack_rims(p, which):
        return dot_nt(
            jnp.concatenate([potential[p, x] for x in which], axis=1),
            jnp.concatenate([rim_ref[:, x * 128 : x * 128 + 128] for x in which], axis=1),
        )

    def both_rims(arrived, p):
        return jnp.where(low_all, arrived[p, 0].astype(jnp.float32), arrived[p, 1].astype(jnp.float32))

    def send_sides(p):
        near["up", p].wait_recv()
        near["down", p].wait_recv()
        added = dot(both_rims(rim_in, p).astype(BF), rim_ref[...])
        for x in range(WIDE):
            slices[p, x] = slices[p, x] + added[:, x * 128 : x * 128 + 128]
        side_out[p, 0] = slices[p, 9].astype(BF)
        side_out[p, 1] = slices[p, 10].astype(BF)
        side_out[p, 2] = slices[p, 0].astype(BF)
        near["right", p] = remote(
            side_out.at[p, pl.ds(0, 2)], side_in.at[p, pl.ds(0, 2)], near_sems, 8 * p + 2, right
        )
        near["left", p] = remote(side_out.at[p, pl.ds(2, 1)], side_in.at[p, pl.ds(2, 1)], near_sems, 8 * p + 3, left)

    def signed(k):
        return jnp.where(k < G // 2, k, k - G).astype(jnp.float32)

    def make_gain():
        fx = signed(brick * 64 + iota((64, G), 0))
        fy = signed(iota((64, G), 1))
        flat = fx * fx + fy * fy

        def one(index, carry):
            fz = signed(slab * 8 + index)
            magnitude = jnp.sqrt(fz * fz + flat)
            scaled = magnitude * (1.0 / BIN) - 8.0
            middle = jnp.exp(-0.5 * scaled * scaled)
            sums = [amp_ref[p, 8] * middle for p in range(2)]
            for way in (1, -1):
                ratio = jnp.exp(way * scaled - 0.5)
                bump = middle
                for center in range(8 + way, 16 if way > 0 else -1, way):
                    bump = bump * ratio
                    ratio = ratio * math.exp(-1.0)
                    sums = [sums[p] + amp_ref[p, center] * bump for p in range(2)]
            for p in range(2):
                gain[p, pl.ds(pl.multiple_of(index * 64, 64), 64), :] = sums[p]
            return carry

        lax.fori_loop(0, 8, one, 0)

    def send(src, dst, u, axis, me, count, sems):
        def one(step, carry):
            peer = lax.rem(me + step, count)
            pltpu.make_async_remote_copy(
                src_ref=src.at[u, peer],
                dst_ref=dst.at[u, me],
                send_sem=sems.at[0, u],
                recv_sem=sems.at[1, u],
                device_id={axis: peer},
                device_id_type=MESH,
            ).start()
            return carry

        lax.fori_loop(1, count, one, 0)

    def send_slabs(make, src, dst, u, sems):
        def to(peer):
            pltpu.make_async_remote_copy(
                src_ref=src.at[u, peer],
                dst_ref=dst.at[u, slab],
                send_sem=sems.at[0, u],
                recv_sem=sems.at[1, u],
                device_id={"slab": peer},
                device_id_type=MESH,
            ).start()

        for dy, dz in CHIP_ORDER:
            pair = lax.rem(slab // 8 + dy, 4) * 4 + lax.rem(slab // 2 + dz, 4)
            make(pair)
            to(2 * pair)
            to(2 * pair + 1)
        make(slab // 2)
        to(slab + 1 - 2 * lax.rem(slab, 2))
        dst[u, slab] = src[u, slab]

    def wait(buf, u, count, sems, which):
        part = buf.at[u, pl.ds(0, count - 1)]
        pltpu.make_async_copy(part, part, sems.at[which, u]).wait()

    def z_pair(p, x):
        rhs = jnp.concatenate([slices[p, x], slices[p, x + 1]], axis=1).astype(BF)
        out = dot(zt[...], rhs)
        for half in range(HALVES):
            for k in range(2):
                lanes = slice(k * 128, k * 128 + 128)
                u = out[half * 256 : half * 256 + 128, lanes]
                v = out[half * 256 + 128 : half * 256 + 256, lanes]
                freq[half, x - 1 + k] = u + turn(v)

    def inner_z(p):
        z_pair(p, 3)
        z_pair(p, 5)

    def outer_z(p):
        near["right", p].wait_recv()
        slices[p, 1] = slices[p, 1] + side_in[p, 0].astype(jnp.float32)
        slices[p, 2] = slices[p, 2] + side_in[p, 1].astype(jnp.float32)
        z_pair(p, 1)
        near["left", p].wait_recv()
        slices[p, 8] = slices[p, 8] + side_in[p, 2].astype(jnp.float32)
        z_pair(p, 7)

        for half in range(HALVES):

            def pack(pair, half=half):
                turned = jnp.swapaxes(freq[half, :, pl.ds(pl.multiple_of(pair * 8, 8), 8), :], 0, 1)
                block[2 * p + half, pl.ds(2 * pair, 2)] = turned.reshape(2, 2, 16, 128).astype(BF)

            send_slabs(pack, block, from_slab, 2 * p + half, slab_sems)

    def x_stage(u):
        wait(from_slab, u, SLABS, slab_sems, 1)
        cols = []
        for two in range(2):
            held = from_slab[u, :, two].astype(jnp.float32)
            cols += [held[:, 0:8].reshape(G, 128), held[:, 8:16].reshape(G, 128)]
        out = dot(xt[...], jnp.concatenate(cols, axis=1).astype(BF))
        for k in range(4):
            lanes = slice(k * 128, k * 128 + 128)
            done = (out[0:G, lanes] + turn(out[G:, lanes])).astype(BF)
            to_brick[u, :, k] = done.reshape(BRICKS, 64, 128)
        send(to_brick, from_brick, u, "brick", brick, BRICKS, brick_sems)
        from_brick[u, brick] = to_brick[u, brick]

    def y_stage(u):
        wait(from_brick, u, BRICKS, brick_sems, 1)
        rows = jnp.concatenate([from_brick[u, b].reshape(G, 128) for b in range(BRICKS)], axis=1)
        spectrum = dot(rows, yt[...])
        weight = gain[u // 2, pl.ds(u % 2 * 256, 256), :]
        filtered = jnp.concatenate([spectrum[:, :G] * weight, spectrum[:, G:] * weight], axis=1)
        back = dot(filtered.astype(BF), iyt[...]).astype(BF)
        for b in range(BRICKS):
            back_brick[u, b] = back[:, b * 128 : b * 128 + 128].reshape(4, 64, 128)
        send(back_brick, got_brick, u, "brick", brick, BRICKS, brick_sems2)
        got_brick[u, brick] = back_brick[u, brick]

    def i_stage(u):
        wait(got_brick, u, BRICKS, brick_sems2, 1)
        after[...] = dot(ixt[...], jnp.concatenate([got_brick[u, :, k].reshape(G, 128) for k in range(4)], axis=1))

        def make(pair):
            at = pl.multiple_of(pair * 16, 16)
            done = []
            for k in range(4):
                lanes = pl.ds(k * 128, 128)
                values = after[pl.ds(at, 16), lanes] - turn(after[pl.ds(G + at, 16), lanes])
                done.append(values.reshape(2, 8, 128))
            for two in range(2):
                back_slab[u, pl.ds(2 * pair, 2), two] = jnp.concatenate(done[2 * two : 2 * two + 2], axis=1).astype(BF)

        send_slabs(make, back_slab, got_slab, u, slab_sems2)

    def home(p):
        for half in range(HALVES):
            wait(got_slab, 2 * p + half, SLABS, slab_sems2, 1)

            def unpack(s, carry, half=half):
                rows = []
                for eight in range(2):
                    held = got_slab[2 * p + half, pl.ds(4 * s + 2 * eight, 2)].astype(jnp.float32)
                    rows.append(jnp.swapaxes(held.reshape(8, 8, 128), 0, 1))
                at = pl.multiple_of(half * 128 + s * 16, 16)
                freq_back[:, pl.ds(at, 16), :] = jnp.concatenate(rows, axis=1).astype(BF)
                return carry

            lax.fori_loop(0, SLABS // 4, unpack, 0, unroll=4)

        def back_z(x):
            out = dot(izt[...], jnp.concatenate([freq_back[x - 1], freq_back[x]], axis=1))
            for k in range(2):
                lanes = slice(k * 128, k * 128 + 128)
                potential[p, x + k] = (out[0:G, lanes] - turn(out[G:, lanes])).astype(BF)

        back_z(1)
        near["left2", p] = remote(
            potential.at[p, pl.ds(1, 2)], potential.at[p, pl.ds(9, 2)], near_sems, 8 * p + 4, left
        )
        back_z(7)
        near["right2", p] = remote(
            potential.at[p, pl.ds(8, 1)], potential.at[p, pl.ds(0, 1)], near_sems, 8 * p + 5, right
        )
        back_z(3)
        back_z(5)
        rim_part[...] = pack_rims(p, range(1, 9))
        place(p, 0)

    def place(p, part):
        def one(step, carry):
            rows = pl.ds(pl.multiple_of(step * 16, 16), 16)
            blank = jnp.zeros((8, 128), jnp.float32)
            turned = []
            for four in range(2):
                tiles = []
                for x in BACK_ORDER[8 * part + 4 * four : 8 * part + 4 * four + 4]:
                    held = potential[p, x, rows, :].astype(jnp.float32)
                    a, b = held[0:8], held[8:16]
                    tiles.append(jnp.where(low_half, a, pltpu.roll(b, 64, 1)))
                    tiles.append(jnp.where(low_half, pltpu.roll(a, 64, 1), b))
                tiles += [blank] * (8 - len(tiles))
                turned.append(jnp.swapaxes(jnp.stack(tiles, axis=0), 0, 1))
            mesh_back[p, pl.ds(step * 8, 8), pl.ds(part * 16, 16), :] = jnp.concatenate(turned, axis=1).astype(BF)
            return carry

        lax.fori_loop(0, 16, one, 0, unroll=4)

    def send_back_rims(p):
        near["left2", p].wait_recv()
        near["right2", p].wait_recv()
        rim_out2[p] = (rim_part[...] + pack_rims(p, (0, 9, 10))).astype(BF)
        near["down2", p] = remote(rim_out2.at[p], rim_in2.at[p, 0], near_sems, 8 * p + 6, down)
        near["up2", p] = remote(rim_out2.at[p], rim_in2.at[p, 1], near_sems, 8 * p + 7, up)
        place(p, 1)
        mesh_back[p, 128] = mesh_back[p, 0]
        mesh_back[p, 129] = mesh_back[p, 1]

    rim_x = iota((BACK_ROWS, LANES), 0) >> 1
    back_x = jnp.where(rim_x < 8, rim_x + 1, jnp.where(rim_x == 8, 0, jnp.where(rim_x < WIDE, rim_x, 99)))
    back_slab_of = iota((BACK_ROWS, LANES), 1) >> 6
    rim_of = iota((WINDOW, 128), 1) >> 5

    def reduce_x(own):
        return own[0:8] + own[8:16] + own[16:24] + own[24:32]

    def read_mesh(p):
        def one(g, carry):
            seen = jnp.zeros((4 * BACK_ROWS, LANES), jnp.float32)
            for z in range(0, 12, 4):
                rows = []
                for i in range(4):
                    at = g * 16 + i * 4 + z // 2
                    rows.append(jnp.concatenate([mesh_back[p, at + side] for side in range(2)], axis=1))
                seen = seen + dot(jnp.concatenate(rows, axis=0), pairs[g, z // 4])
            own = jnp.zeros((BACK_ROWS, LANES), jnp.float32)
            for i in range(4):
                own = own + jnp.where(back_slab_of == i, seen[i * BACK_ROWS : i * BACK_ROWS + BACK_ROWS], 0.0)
            read_ref[:, slot_lanes(g)] = reduce_x(own * line_weights(sorted_ref[:, slot_lanes(g)], back_x))
            return carry

        lax.fori_loop(0, GROUPS, one, 0, unroll=4)

    def read_rims(p):
        near["down2", p].wait_recv()
        near["up2", p].wait_recv()
        rims = both_rims(rim_in2, p)
        rim_near[0:G, :] = rims
        rim_near[G : G + 16, :] = rims[0:16]

        def one(g, carry):
            window = rim_near[pl.ds(pl.multiple_of(g * 32, 16), WINDOW), :]
            window = jnp.concatenate([jnp.where(rim_of == h, window, 0.0) for h in range(3)], axis=0).astype(BF)
            rim = lax.dot_general(
                window, rim_pairs[g], (((0,), (0,)), ((), ())), preferred_element_type=jnp.float32
            )
            own = rim[0:32] + rim[32:64] + rim[64:96]
            readings = reduce_x(own * line_weights(sorted_ref[:, slot_lanes(g)], rim_x)) + read_ref[:, slot_lanes(g)]
            readings = readings + pltpu.roll(readings, 4, 0)
            read_ref[:, slot_lanes(g)] = readings + pltpu.roll(readings, 2, 0)
            return carry

        lax.fori_loop(0, GROUPS, one, 0, unroll=4)

        def unsort(g, total):
            rows = []
            for part in double(read_ref[:, pl.ds(pl.multiple_of(g * 512, 512), 512)]):
                for t in range(4):
                    tile = part[:, t * 128 : t * 128 + 128]
                    rows += [jnp.where(low_half, tile, 0.0), jnp.where(low_half, 0.0, tile)]
            moved = dot(jnp.concatenate(rows, axis=0).astype(BF), rank_ref[...])
            moved = moved[0:64] + moved[64:128]
            for t in range(8):
                total = total + jnp.where(target == g * 8 + t, moved[t * 8 : t * 8 + 8], 0.0)
            return total

        total = lax.fori_loop(0, SLABS // 8, unsort, jnp.zeros((8, atoms), jnp.float32), unroll=4)
        out_ref[p : p + 1, :] = total[0:1]
        out_ref[2 + p : 3 + p, :] = total[1:2]

    spread(0)
    cut(0)
    loads[0].wait()
    send_sides(0)
    for load in loads[1:]:
        load.wait()
    inner_z(0)
    make_gain()
    outer_z(0)
    spread(1)
    cut(1)
    send_sides(1)
    x_stage(0)
    x_stage(1)
    inner_z(1)
    outer_z(1)
    y_stage(0)
    y_stage(1)
    x_stage(2)
    x_stage(3)
    i_stage(0)
    i_stage(1)
    y_stage(2)
    y_stage(3)
    i_stage(2)
    i_stage(3)
    home(0)
    send_back_rims(0)
    home(1)
    read_mesh(0)
    send_back_rims(1)
    read_rims(0)
    read_mesh(1)
    read_rims(1)
    for copy in near.values():
        copy.wait_send()
    for u in range(UNITS):
        wait(block, u, SLABS, slab_sems, 0)
        wait(back_slab, u, SLABS, slab_sems2, 0)
        wait(to_brick, u, BRICKS, brick_sems, 0)
        wait(back_brick, u, BRICKS, brick_sems2, 0)


def body(charges, fractions, inner_cell, dest_slab, filter_amp):
    vmem = pl.BlockSpec(memory_space=pltpu.VMEM)
    anywhere = pl.BlockSpec(memory_space=pl.ANY)
    dma = pltpu.SemaphoreType.DMA
    atoms = charges.shape[1]
    tables = [jnp.asarray(table) for table in make_tables()]
    to_slab = (UNITS, SLABS, 2, 16, 128)
    to_brick = (UNITS, BRICKS, 4, 64, 128)
    return pl.pallas_call(
        kernel,
        out_shape=jax.ShapeDtypeStruct((4, atoms), jnp.float32),
        in_specs=[vmem] * 4 + [pl.BlockSpec(memory_space=pltpu.SMEM)] + [anywhere] * len(tables),
        out_specs=vmem,
        scratch_shapes=[pltpu.VMEM(table.shape, BF) for table in tables]
        + [
            pltpu.VMEM((8, SLABS * CAP), jnp.float32),
            pltpu.VMEM((8, SLABS * CAP), jnp.float32),
            pltpu.VMEM((128, atoms), BF),
            pltpu.VMEM((GROUPS, 3, 256, LANES), BF),
            pltpu.VMEM((GROUPS, 3 * WINDOW, LANES), BF),
            pltpu.VMEM((G + 16, 256), jnp.float32),
            pltpu.VMEM((G + 16, 128), jnp.float32),
            pltpu.VMEM((G, 128), jnp.float32),
            pltpu.VMEM((2, PLACES, ROWS, 128), jnp.float32),
            pltpu.VMEM((2, PLACES, BACK_ROWS, 128), BF),
            pltpu.VMEM((2, WIDE, G, 128), jnp.float32),
            pltpu.VMEM((2, G, 128), BF),
            pltpu.VMEM((2, 2, G, 128), BF),
            pltpu.VMEM((2, G, 128), BF),
            pltpu.VMEM((2, 2, G, 128), BF),
            pltpu.VMEM((2, 3, G, 128), BF),
            pltpu.VMEM((2, 3, G, 128), BF),
            pltpu.VMEM((HALVES, 8, 128, 128), jnp.float32),
            pltpu.VMEM((8, G, 128), BF),
        ]
        + [pltpu.VMEM(to_slab, BF)] * 2
        + [pltpu.VMEM(to_brick, BF)] * 4
        + [pltpu.VMEM(to_slab, BF)] * 2
        + [
            pltpu.VMEM((512, 512), jnp.float32),
            pltpu.VMEM((2, WIDE, G, 128), BF),
            pltpu.VMEM((2, 512, G), jnp.float32),
            dma((len(tables),)),
            dma((2, 16)),
        ]
        + [dma((2, UNITS))] * 4,
        compiler_params=pltpu.CompilerParams(collective_id=0, has_side_effects=True, vmem_limit_bytes=VMEM_LIMIT),
    )(
        charges, fractions, inner_cell.reshape(1, -1), dest_slab.reshape(1, -1), filter_amp, *tables
    )


def solution(mesh):
    in_specs = (
        P(None, ("slab", "brick")),
        P(None, ("slab", "brick")),
        P(("slab", "brick")),
        P(("slab", "brick"), None),
        P(),
    )
    out_specs = P(None, ("slab", "brick"))
    return jax.shard_map(body, mesh=mesh, in_specs=in_specs, out_specs=out_specs, check_vma=False)
```

time: 878 us -> 71.8 us (0.08); the launches traced: 869 us -> 71.5 us
  waiting for transfers between devices: 535 us -> 0 us
  local copies, waits for them, and re-layouts: 142 us -> 1.32 us
  Pallas kernels: 0 us -> 70.2 us
  starting transfers between devices: 70.1 us -> 0 us
  other arithmetic: 55.2 us -> 0 us
  matrix products: 52.5 us -> 0 us
  blocking collectives: 12.8 us -> 0 us
    ppermute x36 -> x0, waiting for transfers between devices: 528 us -> none  [the longest x28 519 us: from_partner(): return lax.ppermute(block, axis, route)]
    pallas_call x0 -> x1, Pallas kernels: none -> 70.2 us  [body(): pl.pallas_call(kernel, out_shape=jax.ShapeDtypeStruct((4, atoms), jnp.flo...]
    ppermute x36 -> x0, starting transfers between devices: 55.6 us -> none  [the longest x28 41.8 us: from_partner(): return lax.ppermute(block, axis, route)]
    dot_general x27 -> x0, matrix products: 52.5 us -> none  [the longest x24 41.1 us: along_axis(): jnp.tensordot(values, matrix_table, axes=([axis_pos], [0]), precision=lax...]
    exp x16 -> x0, local copies, waits for them, and re-layouts: 32.5 us -> none  [bump(): return jnp.exp(-0.5 * scaled * scaled)]
    another operation x5 -> x0, local copies, waits for them, and re-layouts: 24 us -> none  [the longest x1 23.7 us: radial_gain(): jnp.stack([bump(magnitude, float(center), float(BIN)) for center in range...]
    select_n x14 -> x0, other arithmetic: 23.6 us -> none  [the longest x5 13.8 us: forward_section(): jnp.where(is_upper, diff_imag * cosine - diff_real * sine_part, imag_part...]
    convert_element_type x2 -> x0, local copies, waits for them, and re-layouts: 18.1 us -> none  [body(): (weight_z[:, :, None] * weight_y[:, None, :]).reshape(slot_count, -1)]
  transfers between devices with their start and end apart: 38 -> 0, of which waited for: 32 -> 0; matrix products, arithmetic and copies ran while one was open for 12% -> 0% of each run, Pallas kernels for 0% -> 0%
where the time goes in v1:
time: 71.8 us; the launch traced here: 71.5 us
  Pallas kernels  70.2 us (98%)
  local copies, waits for them, and re-layouts  1.32 us (2%)
    pallas_call x1, Pallas kernels, body(): pl.pallas_call(kernel, out_shape=jax.ShapeDtypeStruct((4, atoms), jnp.flo...  70.2 us

profile of v1, /device:TPU:0, one launch (start us, length us, event | category | flops | bytes accessed | tf_op | source)
XLA Modules:
  0.0 71.5 jit_solution(16310962597847897714)
XLA Ops:
  0.0 70.2 %shard_map.118 = f32[4,1024]{1,0:T(4,128)} custom-call(f32[4,1024]{1,0:T(4,128)} %charge_ref.1, f32[3,1024]{1,0:T(4,128)} %frac_ref.1, s32[1,1024]{1,0:T(1,128)} %bitcast.2, s32[1,1024]{1,0:T(1,128)} %bitcast.3, f32[2,16]{1,0:T(2,128)} %amp_ref.1, bf16[128,1408]{1,0:T(8,128)(2,1)} %constant.14.clone.rim_far, bf16[512,256]{1,0:T(8,128)(2,1)} %constant.15.clone.zt_far, ...), custom_call_target="tpu_custom_call" | custom-call | tf_op jit(solution)/shard_map/pallas_call | solution.py:647
  70.2 1.3 %copy.14 = f32[4,1024]{1,0:T(4,128)} copy(f32[4,1024]{1,0:T(4,128)} %shard_map.118) | data formatting | bytes 32768

commit v2 on v1

--- a/solution.py
+++ b/solution.py
@@ -57,9 +57,11 @@
     (2, 2), (0, 1), (1, 0), (0, 3), (3, 0), (1, 2), (2, 1), (3, 2), (2, 3), (0, 2), (2, 0), (1, 1), (3, 3), (1, 3), (3, 1),
 )
 WIDE = 11
+ORDER = (1, 2, 3, 4, 5, 6, 7, 8, 0, 9, 10)
+SIDES = (9, 10, 0)
+EDGES = (1, 2, 8)
 ROWS = 24
 BACK_ROWS = 32
-BACK_ORDER = (1, 2, 3, 4, 5, 6, 7, 8, 0, 9, 10)
 VMEM_LIMIT = 56 * 1024 * 1024
 
 
@@ -69,10 +71,10 @@
 
 def rim_table():
     table = np.zeros((128, WIDE, 2, 64), np.float32)
-    for x in range(WIDE):
+    for at, x in enumerate(ORDER):
         for r in range(2):
             for start, y in ((0, 0), (32, 1), (64, 63)):
-                table[start + x * 2 + r, x, r, y] = 1.0
+                table[start + at * 2 + r, x, r, y] = 1.0
     return table.reshape(128, WIDE * 128)
 
 
@@ -112,8 +114,7 @@
     return high, values - high
 
 
-def dense(cell, fraction, places):
-    weights = spline_weights(fraction)
+def dense(cell, weights, places):
     total = 0.0
     for j in range(4):
         total = total + jnp.where(places == cell + j, weights[j], 0.0)
@@ -124,9 +125,9 @@
     return pl.ds(pl.multiple_of(g * LANES, LANES), LANES)
 
 
-def line_weights(held, places):
-    code = held[7:8, :].astype(jnp.int32)
-    return dense((code >> 3) & 7, held[6:7, :], places)
+def row_x(shape):
+    at = iota(shape, 0) >> 1
+    return jnp.where(at < 8, at + 1, jnp.where(at == 8, 0, jnp.where(at < WIDE, at, 99)))
 
 
 def remote(src, dst, sems, at, target):
@@ -147,7 +148,7 @@
     rim_far, zt_far, xt_far, yt_far, iyt_far, ixt_far, izt_far,
     out_ref,
     rim_ref, zt, xt, yt, iyt, ixt, izt,
-    sorted_ref, read_ref, rank_ref, pairs, rim_pairs, rim_sums, rim_near, rim_part, mesh, mesh_back, slices,
+    sorted_ref, spline_ref, line_ref, read_ref, rank_ref, pairs, rim_pairs, rim_sums, rim_near, rim_part, mesh, mesh_back, added, edges, slices,
     rim_out, rim_in, rim_out2, rim_in2, side_out, side_in, freq, freq_back,
     block, from_slab, to_brick, from_brick, back_brick, got_brick, back_slab, got_slab, after, potential, gain,
     table_sems, near_sems, slab_sems, brick_sems, brick_sems2, slab_sems2,
@@ -211,12 +212,18 @@
 
     lax.fori_loop(0, SLABS // 8, sort, 0, unroll=4)
 
+    for j, weight in enumerate(spline_weights(sorted_ref[4:7, :])):
+        spline_ref[j, 0:3, :] = weight
+
+    def along(dim, g):
+        return [spline_ref[j, dim : dim + 1, slot_lanes(g)] for j in range(4)]
+
     slab_of = iota((ROWS, LANES), 1) >> 6
-    x_of = iota((ROWS, LANES), 0) >> 1
     first_part = (iota((ROWS, LANES), 0) & 1) == 0
-
-    def line(held, p):
-        return jnp.where(first_part, held[p : p + 1, :], held[2 + p : 3 + p, :]) * line_weights(held, x_of)
+    x_of = row_x((BACK_ROWS, LANES))
+
+    def line(held, g, p):
+        return jnp.where(first_part, held[p : p + 1, :], held[2 + p : 3 + p, :]) * line_ref[g, 0:ROWS, :]
 
     rim_sums[...] = jnp.zeros(rim_sums.shape, jnp.float32)
     window_row = iota((WINDOW, LANES), 0)
@@ -226,11 +233,12 @@
     def make_rims(g, carry):
         held = sorted_ref[:, slot_lanes(g)]
         code = held[7:8, :].astype(jnp.int32)
-        wz = dense((code & 7) + slab_start, held[4:5, :], window_place)
-        lines = [line(held, p) for p in range(2)]
+        line_ref[g] = dense((code >> 3) & 7, along(2, g), x_of)
+        wz = dense((code & 7) + slab_start, along(0, g), window_place)
+        lines = [line(held, g, p) for p in range(2)]
         blocks, columns = [], []
         for h, y in enumerate((64, 65, -1)):
-            rim = (wz * dense((code >> 6) - 1, held[5:6, :], y)).astype(BF)
+            rim = (wz * dense((code >> 6) - 1, along(1, g), y)).astype(BF)
             rim_pairs[g, pl.ds(h * WINDOW, WINDOW), :] = rim
             blocks.append(rim)
             rows = []
@@ -262,9 +270,9 @@
             held = sorted_ref[:, slot_lanes(g)]
             if p == 0:
                 code = held[7:8, :].astype(jnp.int32)
-                wz = dense(code & 7, held[4:5, :], iota((16, LANES), 0))
-                wy = dense((code >> 6) - 1, held[5:6, :], iota((64, LANES), 0))
-            own = line(held, p)
+                wz = dense(code & 7, along(0, g), iota((16, LANES), 0))
+                wy = dense((code >> 6) - 1, along(1, g), iota((64, LANES), 0))
+            own = line(held, g, p)
             lines = jnp.concatenate([jnp.where(slab_of == i, own, 0.0) for i in range(4)], axis=0).astype(BF)
             for z in (4, 8, 0):
                 if p == 0:
@@ -289,41 +297,43 @@
     def turn(values):
         return sign[0 : values.shape[0]] * pltpu.roll(values, 64, 1)
 
+    def pack_rims(p, which):
+        return dot_nt(
+            jnp.concatenate([potential[p, x] for x in which], axis=1),
+            jnp.concatenate([rim_ref[:, x * 128 : x * 128 + 128] for x in which], axis=1),
+        )
+
+    def both_rims(arrived, p):
+        return jnp.where(low_all, arrived[p, 0].astype(jnp.float32), arrived[p, 1].astype(jnp.float32))
+
     def cut(p):
+        near["up", p].wait_recv()
+        near["down", p].wait_recv()
+        added[...] = dot(both_rims(rim_in, p).astype(BF), rim_ref[...]).astype(BF)
+
         def one(step, carry):
+            rows = pl.ds(pl.multiple_of(step * 16, 16), 16)
             for part in range(3):
                 turned = jnp.swapaxes(mesh[p, pl.ds(step * 8, 8), pl.ds(part * 8, 8), :], 0, 1)
-                for x in range(4 * part, min(4 * part + 4, WIDE)):
-                    a, b = turned[x % 4 * 2], turned[x % 4 * 2 + 1]
-                    slices[p, x, pl.ds(pl.multiple_of(step * 16, 16), 16), :] = jnp.concatenate(
+                for at, x in enumerate(ORDER[4 * part : 4 * part + 4]):
+                    a, b = turned[2 * at], turned[2 * at + 1]
+                    core = jnp.concatenate(
                         [
                             jnp.where(low_half, a, pltpu.roll(b, 64, 1)),
                             jnp.where(low_half, pltpu.roll(a, 64, 1), b),
                         ],
                         axis=0,
                     )
+                    core = core + added[rows, pl.ds(x * 128, 128)].astype(jnp.float32)
+                    if x in SIDES:
+                        side_out[p, SIDES.index(x), rows, :] = core.astype(BF)
+                    elif x in EDGES:
+                        edges[p, EDGES.index(x), rows, :] = core
+                    else:
+                        slices[p, x, rows, :] = core.astype(BF)
             return carry
 
         lax.fori_loop(0, 16, one, 0, unroll=2)
-
-    def pack_rims(p, which):
-        return dot_nt(
-            jnp.concatenate([potential[p, x] for x in which], axis=1),
-            jnp.concatenate([rim_ref[:, x * 128 : x * 128 + 128] for x in which], axis=1),
-        )
-
-    def both_rims(arrived, p):
-        return jnp.where(low_all, arrived[p, 0].astype(jnp.float32), arrived[p, 1].astype(jnp.float32))
-
-    def send_sides(p):
-        near["up", p].wait_recv()
-        near["down", p].wait_recv()
-        added = dot(both_rims(rim_in, p).astype(BF), rim_ref[...])
-        for x in range(WIDE):
-            slices[p, x] = slices[p, x] + added[:, x * 128 : x * 128 + 128]
-        side_out[p, 0] = slices[p, 9].astype(BF)
-        side_out[p, 1] = slices[p, 10].astype(BF)
-        side_out[p, 2] = slices[p, 0].astype(BF)
         near["right", p] = remote(
             side_out.at[p, pl.ds(0, 2)], side_in.at[p, pl.ds(0, 2)], near_sems, 8 * p + 2, right
         )
@@ -396,8 +406,7 @@
         pltpu.make_async_copy(part, part, sems.at[which, u]).wait()
 
     def z_pair(p, x):
-        rhs = jnp.concatenate([slices[p, x], slices[p, x + 1]], axis=1).astype(BF)
-        out = dot(zt[...], rhs)
+        out = dot(zt[...], jnp.concatenate([slices[p, x], slices[p, x + 1]], axis=1))
         for half in range(HALVES):
             for k in range(2):
                 lanes = slice(k * 128, k * 128 + 128)
@@ -411,13 +420,12 @@
 
     def outer_z(p):
         near["right", p].wait_recv()
-        slices[p, 1] = slices[p, 1] + side_in[p, 0].astype(jnp.float32)
-        slices[p, 2] = slices[p, 2] + side_in[p, 1].astype(jnp.float32)
+        for at in range(2):
+            slices[p, EDGES[at]] = (edges[p, at] + side_in[p, at].astype(jnp.float32)).astype(BF)
         z_pair(p, 1)
         near["left", p].wait_recv()
-        slices[p, 8] = slices[p, 8] + side_in[p, 2].astype(jnp.float32)
+        slices[p, EDGES[2]] = (edges[p, 2] + side_in[p, 2].astype(jnp.float32)).astype(BF)
         z_pair(p, 7)
-
         for half in range(HALVES):
 
             def pack(pair, half=half):
@@ -508,8 +516,11 @@
             blank = jnp.zeros((8, 128), jnp.float32)
             turned = []
             for four in range(2):
+                if 8 * part + 4 * four >= WIDE:
+                    turned.append(jnp.zeros((8, 8, 128), jnp.float32))
+                    continue
                 tiles = []
-                for x in BACK_ORDER[8 * part + 4 * four : 8 * part + 4 * four + 4]:
+                for x in ORDER[8 * part + 4 * four : 8 * part + 4 * four + 4]:
                     held = potential[p, x, rows, :].astype(jnp.float32)
                     a, b = held[0:8], held[8:16]
                     tiles.append(jnp.where(low_half, a, pltpu.roll(b, 64, 1)))
@@ -531,8 +542,6 @@
         mesh_back[p, 128] = mesh_back[p, 0]
         mesh_back[p, 129] = mesh_back[p, 1]
 
-    rim_x = iota((BACK_ROWS, LANES), 0) >> 1
-    back_x = jnp.where(rim_x < 8, rim_x + 1, jnp.where(rim_x == 8, 0, jnp.where(rim_x < WIDE, rim_x, 99)))
     back_slab_of = iota((BACK_ROWS, LANES), 1) >> 6
     rim_of = iota((WINDOW, 128), 1) >> 5
 
@@ -551,7 +560,7 @@
             own = jnp.zeros((BACK_ROWS, LANES), jnp.float32)
             for i in range(4):
                 own = own + jnp.where(back_slab_of == i, seen[i * BACK_ROWS : i * BACK_ROWS + BACK_ROWS], 0.0)
-            read_ref[:, slot_lanes(g)] = reduce_x(own * line_weights(sorted_ref[:, slot_lanes(g)], back_x))
+            read_ref[:, slot_lanes(g)] = reduce_x(own * line_ref[g])
             return carry
 
         lax.fori_loop(0, GROUPS, one, 0, unroll=4)
@@ -570,7 +579,7 @@
                 window, rim_pairs[g], (((0,), (0,)), ((), ())), preferred_element_type=jnp.float32
             )
             own = rim[0:32] + rim[32:64] + rim[64:96]
-            readings = reduce_x(own * line_weights(sorted_ref[:, slot_lanes(g)], rim_x)) + read_ref[:, slot_lanes(g)]
+            readings = reduce_x(own * line_ref[g]) + read_ref[:, slot_lanes(g)]
             readings = readings + pltpu.roll(readings, 4, 0)
             read_ref[:, slot_lanes(g)] = readings + pltpu.roll(readings, 2, 0)
             return carry
@@ -594,9 +603,8 @@
         out_ref[2 + p : 3 + p, :] = total[1:2]
 
     spread(0)
+    loads[0].wait()
     cut(0)
-    loads[0].wait()
-    send_sides(0)
     for load in loads[1:]:
         load.wait()
     inner_z(0)
@@ -604,7 +612,6 @@
     outer_z(0)
     spread(1)
     cut(1)
-    send_sides(1)
     x_stage(0)
     x_stage(1)
     inner_z(1)
@@ -652,6 +659,8 @@
         scratch_shapes=[pltpu.VMEM(table.shape, BF) for table in tables]
         + [
             pltpu.VMEM((8, SLABS * CAP), jnp.float32),
+            pltpu.VMEM((4, 8, SLABS * CAP), jnp.float32),
+            pltpu.VMEM((GROUPS, BACK_ROWS, LANES), jnp.float32),
             pltpu.VMEM((8, SLABS * CAP), jnp.float32),
             pltpu.VMEM((128, atoms), BF),
             pltpu.VMEM((GROUPS, 3, 256, LANES), BF),
@@ -661,7 +670,9 @@
             pltpu.VMEM((G, 128), jnp.float32),
             pltpu.VMEM((2, PLACES, ROWS, 128), jnp.float32),
             pltpu.VMEM((2, PLACES, BACK_ROWS, 128), BF),
-            pltpu.VMEM((2, WIDE, G, 128), jnp.float32),
+            pltpu.VMEM((G, WIDE * 128), BF),
+            pltpu.VMEM((2, 3, G, 128), jnp.float32),
+            pltpu.VMEM((2, WIDE, G, 128), BF),
             pltpu.VMEM((2, G, 128), BF),
             pltpu.VMEM((2, 2, G, 128), BF),
             pltpu.VMEM((2, G, 128), BF),

time: 71.8 us -> 72.6 us (1.011)
  Pallas kernels: 70.2 us -> 71 us
    pallas_call x1, Pallas kernels: 70.2 us -> 71 us  [body(): pl.pallas_call(kernel, out_shape=jax.ShapeDtypeStruct((4, atoms), jnp.flo...]
where the time goes in v2:
time: 72.6 us; the launch traced here: 72.4 us
  Pallas kernels  71 us (98%)
  local copies, waits for them, and re-layouts  1.32 us (2%)
    pallas_call x1, Pallas kernels, body(): pl.pallas_call(kernel, out_shape=jax.ShapeDtypeStruct((4, atoms), jnp.flo...  71 us

profile of v2, /device:TPU:0, one launch (start us, length us, event | category | flops | bytes accessed | tf_op | source)
XLA Modules:
  0.0 72.4 jit_solution(10052300760283745541)
XLA Ops:
  0.0 71.0 %shard_map.118 = f32[4,1024]{1,0:T(4,128)} custom-call(f32[4,1024]{1,0:T(4,128)} %charge_ref.1, f32[3,1024]{1,0:T(4,128)} %frac_ref.1, s32[1,1024]{1,0:T(1,128)} %bitcast.2, s32[1,1024]{1,0:T(1,128)} %bitcast.3, f32[2,16]{1,0:T(2,128)} %amp_ref.1, bf16[128,1408]{1,0:T(8,128)(2,1)} %constant.14.clone.rim_far, bf16[512,256]{1,0:T(8,128)(2,1)} %constant.15.clone.zt_far, ...), custom_call_target="tpu_custom_call" | custom-call | tf_op jit(solution)/shard_map/pallas_call | solution.py:654
  71.0 1.3 %copy.14 = f32[4,1024]{1,0:T(4,128)} copy(f32[4,1024]{1,0:T(4,128)} %shard_map.118) | data formatting | bytes 32768

commit v3 on v2

--- a/solution.py
+++ b/solution.py
@@ -148,7 +148,7 @@
     rim_far, zt_far, xt_far, yt_far, iyt_far, ixt_far, izt_far,
     out_ref,
     rim_ref, zt, xt, yt, iyt, ixt, izt,
-    sorted_ref, spline_ref, line_ref, read_ref, rank_ref, pairs, rim_pairs, rim_sums, rim_near, rim_part, mesh, mesh_back, added, edges, slices,
+    sorted_ref, spline_ref, line_ref, read_ref, rank_ref, pairs, rim_pairs, rim_sums, rim_near, rim_part, mesh, mesh_back, slices,
     rim_out, rim_in, rim_out2, rim_in2, side_out, side_in, freq, freq_back,
     block, from_slab, to_brick, from_brick, back_brick, got_brick, back_slab, got_slab, after, potential, gain,
     table_sems, near_sems, slab_sems, brick_sems, brick_sems2, slab_sems2,
@@ -253,7 +253,7 @@
         )
         return carry
 
-    lax.fori_loop(0, GROUPS, make_rims, 0, unroll=4)
+    lax.fori_loop(0, GROUPS, make_rims, 0, unroll=8)
     rim_sums[0:16, :] = rim_sums[0:16, :] + rim_sums[G : G + 16, :]
     near = {}
     for p in range(2):
@@ -287,7 +287,7 @@
                         mesh[p, at] = part if z else mesh[p, at] + part
             return carry
 
-        lax.fori_loop(0, GROUPS, one, 0, unroll=4)
+        lax.fori_loop(0, GROUPS, one, 0, unroll=8)
         mesh[p, 0] = mesh[p, 0] + mesh[p, 128]
         mesh[p, 1] = mesh[p, 1] + mesh[p, 129]
 
@@ -307,37 +307,36 @@
         return jnp.where(low_all, arrived[p, 0].astype(jnp.float32), arrived[p, 1].astype(jnp.float32))
 
     def cut(p):
-        near["up", p].wait_recv()
-        near["down", p].wait_recv()
-        added[...] = dot(both_rims(rim_in, p).astype(BF), rim_ref[...]).astype(BF)
-
         def one(step, carry):
-            rows = pl.ds(pl.multiple_of(step * 16, 16), 16)
             for part in range(3):
                 turned = jnp.swapaxes(mesh[p, pl.ds(step * 8, 8), pl.ds(part * 8, 8), :], 0, 1)
                 for at, x in enumerate(ORDER[4 * part : 4 * part + 4]):
                     a, b = turned[2 * at], turned[2 * at + 1]
-                    core = jnp.concatenate(
+                    slices[p, x, pl.ds(pl.multiple_of(step * 16, 16), 16), :] = jnp.concatenate(
                         [
                             jnp.where(low_half, a, pltpu.roll(b, 64, 1)),
                             jnp.where(low_half, pltpu.roll(a, 64, 1), b),
                         ],
                         axis=0,
                     )
-                    core = core + added[rows, pl.ds(x * 128, 128)].astype(jnp.float32)
-                    if x in SIDES:
-                        side_out[p, SIDES.index(x), rows, :] = core.astype(BF)
-                    elif x in EDGES:
-                        edges[p, EDGES.index(x), rows, :] = core
-                    else:
-                        slices[p, x, rows, :] = core.astype(BF)
             return carry
 
-        lax.fori_loop(0, 16, one, 0, unroll=2)
+        lax.fori_loop(0, 16, one, 0, unroll=8)
+
+    def send_sides(p):
+        near["up", p].wait_recv()
+        near["down", p].wait_recv()
+        rims = both_rims(rim_in, p).astype(BF)
+        added = dot(rims, jnp.concatenate([rim_ref[:, x * 128 : x * 128 + 128] for x in SIDES], axis=1))
+        for at, x in enumerate(SIDES):
+            side_out[p, at] = (slices[p, x] + added[:, at * 128 : at * 128 + 128]).astype(BF)
         near["right", p] = remote(
             side_out.at[p, pl.ds(0, 2)], side_in.at[p, pl.ds(0, 2)], near_sems, 8 * p + 2, right
         )
         near["left", p] = remote(side_out.at[p, pl.ds(2, 1)], side_in.at[p, pl.ds(2, 1)], near_sems, 8 * p + 3, left)
+        added = dot(rims, rim_ref[:, 128 : 9 * 128])
+        for x in range(1, 9):
+            slices[p, x] = slices[p, x] + added[:, x * 128 - 128 : x * 128]
 
     def signed(k):
         return jnp.where(k < G // 2, k, k - G).astype(jnp.float32)
@@ -364,7 +363,7 @@
                 gain[p, pl.ds(pl.multiple_of(index * 64, 64), 64), :] = sums[p]
             return carry
 
-        lax.fori_loop(0, 8, one, 0)
+        lax.fori_loop(0, 8, one, 0, unroll=2)
 
     def send(src, dst, u, axis, me, count, sems):
         def one(step, carry):
@@ -406,7 +405,7 @@
         pltpu.make_async_copy(part, part, sems.at[which, u]).wait()
 
     def z_pair(p, x):
-        out = dot(zt[...], jnp.concatenate([slices[p, x], slices[p, x + 1]], axis=1))
+        out = dot(zt[...], jnp.concatenate([slices[p, x], slices[p, x + 1]], axis=1).astype(BF))
         for half in range(HALVES):
             for k in range(2):
                 lanes = slice(k * 128, k * 128 + 128)
@@ -421,10 +420,10 @@
     def outer_z(p):
         near["right", p].wait_recv()
         for at in range(2):
-            slices[p, EDGES[at]] = (edges[p, at] + side_in[p, at].astype(jnp.float32)).astype(BF)
+            slices[p, EDGES[at]] = slices[p, EDGES[at]] + side_in[p, at].astype(jnp.float32)
         z_pair(p, 1)
         near["left", p].wait_recv()
-        slices[p, EDGES[2]] = (edges[p, 2] + side_in[p, 2].astype(jnp.float32)).astype(BF)
+        slices[p, EDGES[2]] = slices[p, EDGES[2]] + side_in[p, 2].astype(jnp.float32)
         z_pair(p, 7)
         for half in range(HALVES):
 
@@ -489,7 +488,7 @@
                 freq_back[:, pl.ds(at, 16), :] = jnp.concatenate(rows, axis=1).astype(BF)
                 return carry
 
-            lax.fori_loop(0, SLABS // 4, unpack, 0, unroll=4)
+            lax.fori_loop(0, SLABS // 4, unpack, 0, unroll=8)
 
         def back_z(x):
             out = dot(izt[...], jnp.concatenate([freq_back[x - 1], freq_back[x]], axis=1))
@@ -530,7 +529,7 @@
             mesh_back[p, pl.ds(step * 8, 8), pl.ds(part * 16, 16), :] = jnp.concatenate(turned, axis=1).astype(BF)
             return carry
 
-        lax.fori_loop(0, 16, one, 0, unroll=4)
+        lax.fori_loop(0, 16, one, 0, unroll=8)
 
     def send_back_rims(p):
         near["left2", p].wait_recv()
@@ -563,7 +562,7 @@
             read_ref[:, slot_lanes(g)] = reduce_x(own * line_ref[g])
             return carry
 
-        lax.fori_loop(0, GROUPS, one, 0, unroll=4)
+        lax.fori_loop(0, GROUPS, one, 0, unroll=8)
 
     def read_rims(p):
         near["down2", p].wait_recv()
@@ -584,7 +583,7 @@
             read_ref[:, slot_lanes(g)] = readings + pltpu.roll(readings, 2, 0)
             return carry
 
-        lax.fori_loop(0, GROUPS, one, 0, unroll=4)
+        lax.fori_loop(0, GROUPS, one, 0, unroll=8)
 
         def unsort(g, total):
             rows = []
@@ -603,8 +602,9 @@
         out_ref[2 + p : 3 + p, :] = total[1:2]
 
     spread(0)
+    cut(0)
     loads[0].wait()
-    cut(0)
+    send_sides(0)
     for load in loads[1:]:
         load.wait()
     inner_z(0)
@@ -612,6 +612,7 @@
     outer_z(0)
     spread(1)
     cut(1)
+    send_sides(1)
     x_stage(0)
     x_stage(1)
     inner_z(1)
@@ -670,9 +671,7 @@
             pltpu.VMEM((G, 128), jnp.float32),
             pltpu.VMEM((2, PLACES, ROWS, 128), jnp.float32),
             pltpu.VMEM((2, PLACES, BACK_ROWS, 128), BF),
-            pltpu.VMEM((G, WIDE * 128), BF),
-            pltpu.VMEM((2, 3, G, 128), jnp.float32),
-            pltpu.VMEM((2, WIDE, G, 128), BF),
+            pltpu.VMEM((2, WIDE, G, 128), jnp.float32),
             pltpu.VMEM((2, G, 128), BF),
             pltpu.VMEM((2, 2, G, 128), BF),
             pltpu.VMEM((2, G, 128), BF),

time: 72.6 us -> 71.6 us (0.986)
  Pallas kernels: 71 us -> 70 us
    pallas_call x1, Pallas kernels: 71 us -> 70 us  [body(): pl.pallas_call(kernel, out_shape=jax.ShapeDtypeStruct((4, atoms), jnp.flo...]
where the time goes in v3:
time: 71.6 us; the launch traced here: 71.4 us
  Pallas kernels  70 us (98%)
  local copies, waits for them, and re-layouts  1.32 us (2%)
    pallas_call x1, Pallas kernels, body(): pl.pallas_call(kernel, out_shape=jax.ShapeDtypeStruct((4, atoms), jnp.flo...  70 us

profile of v3, /device:TPU:0, one launch (start us, length us, event | category | flops | bytes accessed | tf_op | source)
XLA Modules:
  0.0 71.4 jit_solution(7790000856089980810)
XLA Ops:
  0.0 70.0 %shard_map.118 = f32[4,1024]{1,0:T(4,128)} custom-call(f32[4,1024]{1,0:T(4,128)} %charge_ref.1, f32[3,1024]{1,0:T(4,128)} %frac_ref.1, s32[1,1024]{1,0:T(1,128)} %bitcast.2, s32[1,1024]{1,0:T(1,128)} %bitcast.3, f32[2,16]{1,0:T(2,128)} %amp_ref.1, bf16[128,1408]{1,0:T(8,128)(2,1)} %constant.14.clone.rim_far, bf16[512,256]{1,0:T(8,128)(2,1)} %constant.15.clone.zt_far, ...), custom_call_target="tpu_custom_call" | custom-call | tf_op jit(solution)/shard_map/pallas_call | solution.py:655
  70.1 1.3 %copy.14 = f32[4,1024]{1,0:T(4,128)} copy(f32[4,1024]{1,0:T(4,128)} %shard_map.118) | data formatting | bytes 32768

commit v4 on v3

--- a/solution.py
+++ b/solution.py
@@ -52,7 +52,10 @@
 PLACES = 132
 WINDOW = 48
 HALVES = 2
-UNITS = 4
+UNITS = 6
+PAIR_OF = (0, 0, 0, 1, 1, 1)
+TILES = ((0, 1), (1, 2), (2, 4), (0, 2), (2, 3), (3, 4))
+UNITS_OF = ((0, 1, 2), (3, 4, 5))
 CHIP_ORDER = (
     (2, 2), (0, 1), (1, 0), (0, 3), (3, 0), (1, 2), (2, 1), (3, 2), (2, 3), (0, 2), (2, 0), (1, 1), (3, 3), (1, 3), (3, 1),
 )
@@ -365,26 +368,39 @@
 
         lax.fori_loop(0, 8, one, 0, unroll=2)
 
-    def send(src, dst, u, axis, me, count, sems):
-        def one(step, carry):
-            peer = lax.rem(me + step, count)
+    def tiles_of(u):
+        return pl.ds(TILES[u][0], TILES[u][1] - TILES[u][0])
+
+    def freqs_of(u):
+        return pl.ds(2 * TILES[u][0], 2 * (TILES[u][1] - TILES[u][0]))
+
+    def send_bricks(src, dst, u, sems):
+        p = PAIR_OF[u]
+        for step in range(1, BRICKS):
+            peer = lax.rem(brick + step, BRICKS)
             pltpu.make_async_remote_copy(
-                src_ref=src.at[u, peer],
-                dst_ref=dst.at[u, me],
+                src_ref=src.at[p, peer, freqs_of(u)],
+                dst_ref=dst.at[p, brick, freqs_of(u)],
                 send_sem=sems.at[0, u],
                 recv_sem=sems.at[1, u],
-                device_id={axis: peer},
+                device_id={"brick": peer},
                 device_id_type=MESH,
             ).start()
-            return carry
-
-        lax.fori_loop(1, count, one, 0)
+        dst[p, brick, freqs_of(u)] = src[p, brick, freqs_of(u)]
+
+    def wait_bricks(buf, u, sem):
+        part = buf.at[PAIR_OF[u], pl.ds(0, BRICKS - 1), freqs_of(u)]
+        pltpu.make_async_copy(part, part, sem).wait()
+
+    def wait_slabs(buf, u, sem):
+        part = buf.at[PAIR_OF[u], pl.ds(0, SLABS - 1), tiles_of(u)]
+        pltpu.make_async_copy(part, part, sem).wait()
 
     def send_slabs(make, src, dst, u, sems):
         def to(peer):
             pltpu.make_async_remote_copy(
-                src_ref=src.at[u, peer],
-                dst_ref=dst.at[u, slab],
+                src_ref=src.at[PAIR_OF[u], peer, tiles_of(u)],
+                dst_ref=dst.at[PAIR_OF[u], slab, tiles_of(u)],
                 send_sem=sems.at[0, u],
                 recv_sem=sems.at[1, u],
                 device_id={"slab": peer},
@@ -398,11 +414,7 @@
             to(2 * pair + 1)
         make(slab // 2)
         to(slab + 1 - 2 * lax.rem(slab, 2))
-        dst[u, slab] = src[u, slab]
-
-    def wait(buf, u, count, sems, which):
-        part = buf.at[u, pl.ds(0, count - 1)]
-        pltpu.make_async_copy(part, part, sems.at[which, u]).wait()
+        dst[PAIR_OF[u], slab, tiles_of(u)] = src[PAIR_OF[u], slab, tiles_of(u)]
 
     def z_pair(p, x):
         out = dot(zt[...], jnp.concatenate([slices[p, x], slices[p, x + 1]], axis=1).astype(BF))
@@ -425,64 +437,83 @@
         near["left", p].wait_recv()
         slices[p, EDGES[2]] = slices[p, EDGES[2]] + side_in[p, 2].astype(jnp.float32)
         z_pair(p, 7)
-        for half in range(HALVES):
-
-            def pack(pair, half=half):
-                turned = jnp.swapaxes(freq[half, :, pl.ds(pl.multiple_of(pair * 8, 8), 8), :], 0, 1)
-                block[2 * p + half, pl.ds(2 * pair, 2)] = turned.reshape(2, 2, 16, 128).astype(BF)
-
-            send_slabs(pack, block, from_slab, 2 * p + half, slab_sems)
+
+        def pack(halves):
+            def one(pair):
+                for half in halves:
+                    turned = jnp.swapaxes(freq[half, :, pl.ds(pl.multiple_of(pair * 8, 8), 8), :], 0, 1)
+                    block[p, pl.ds(2 * pair, 2), pl.ds(2 * half, 2)] = turned.reshape(2, 2, 16, 128).astype(BF)
+
+            return one
+
+        made = 0
+        for u in UNITS_OF[p]:
+            needed = (TILES[u][1] + 1) // 2
+            send_slabs(pack(range(made, needed)), block, from_slab, u, slab_sems)
+            made = needed
 
     def x_stage(u):
-        wait(from_slab, u, SLABS, slab_sems, 1)
+        wait_slabs(from_slab, u, slab_sems.at[1, u])
+        p = PAIR_OF[u]
         cols = []
-        for two in range(2):
-            held = from_slab[u, :, two].astype(jnp.float32)
+        for tile in range(*TILES[u]):
+            held = from_slab[p, :, tile].astype(jnp.float32)
             cols += [held[:, 0:8].reshape(G, 128), held[:, 8:16].reshape(G, 128)]
         out = dot(xt[...], jnp.concatenate(cols, axis=1).astype(BF))
-        for k in range(4):
+        for k in range(len(cols)):
             lanes = slice(k * 128, k * 128 + 128)
             done = (out[0:G, lanes] + turn(out[G:, lanes])).astype(BF)
-            to_brick[u, :, k] = done.reshape(BRICKS, 64, 128)
-        send(to_brick, from_brick, u, "brick", brick, BRICKS, brick_sems)
-        from_brick[u, brick] = to_brick[u, brick]
+            to_brick[p, :, 2 * TILES[u][0] + k] = done.reshape(BRICKS, 64, 128)
+        send_bricks(to_brick, from_brick, u, brick_sems)
 
     def y_stage(u):
-        wait(from_brick, u, BRICKS, brick_sems, 1)
-        rows = jnp.concatenate([from_brick[u, b].reshape(G, 128) for b in range(BRICKS)], axis=1)
+        wait_bricks(from_brick, u, brick_sems.at[1, u])
+        p = PAIR_OF[u]
+        first, count = 2 * TILES[u][0], 2 * (TILES[u][1] - TILES[u][0])
+        rows = jnp.concatenate(
+            [from_brick[p, b, freqs_of(u)].reshape(count * 64, 128) for b in range(BRICKS)], axis=1
+        )
         spectrum = dot(rows, yt[...])
-        weight = gain[u // 2, pl.ds(u % 2 * 256, 256), :]
+        weight = gain[p, pl.ds(first * 64, count * 64), :]
         filtered = jnp.concatenate([spectrum[:, :G] * weight, spectrum[:, G:] * weight], axis=1)
         back = dot(filtered.astype(BF), iyt[...]).astype(BF)
         for b in range(BRICKS):
-            back_brick[u, b] = back[:, b * 128 : b * 128 + 128].reshape(4, 64, 128)
-        send(back_brick, got_brick, u, "brick", brick, BRICKS, brick_sems2)
-        got_brick[u, brick] = back_brick[u, brick]
+            back_brick[p, b, freqs_of(u)] = back[:, b * 128 : b * 128 + 128].reshape(count, 64, 128)
+        send_bricks(back_brick, got_brick, u, brick_sems2)
 
     def i_stage(u):
-        wait(got_brick, u, BRICKS, brick_sems2, 1)
-        after[...] = dot(ixt[...], jnp.concatenate([got_brick[u, :, k].reshape(G, 128) for k in range(4)], axis=1))
+        wait_bricks(got_brick, u, brick_sems2.at[1, u])
+        p = PAIR_OF[u]
+        first, last = 2 * TILES[u][0], 2 * TILES[u][1]
+        after[:, 0 : (last - first) * 128] = dot(
+            ixt[...], jnp.concatenate([got_brick[p, :, k].reshape(G, 128) for k in range(first, last)], axis=1)
+        )
 
         def make(pair):
             at = pl.multiple_of(pair * 16, 16)
             done = []
-            for k in range(4):
+            for k in range(last - first):
                 lanes = pl.ds(k * 128, 128)
                 values = after[pl.ds(at, 16), lanes] - turn(after[pl.ds(G + at, 16), lanes])
                 done.append(values.reshape(2, 8, 128))
-            for two in range(2):
-                back_slab[u, pl.ds(2 * pair, 2), two] = jnp.concatenate(done[2 * two : 2 * two + 2], axis=1).astype(BF)
+            for tile in range(*TILES[u]):
+                two = 2 * tile - first
+                back_slab[p, pl.ds(2 * pair, 2), tile] = jnp.concatenate(done[two : two + 2], axis=1).astype(BF)
 
         send_slabs(make, back_slab, got_slab, u, slab_sems2)
 
     def home(p):
+        there = 0
         for half in range(HALVES):
-            wait(got_slab, 2 * p + half, SLABS, slab_sems2, 1)
+            for u in UNITS_OF[p]:
+                if there < 2 * half + 2 and there == TILES[u][0]:
+                    wait_slabs(got_slab, u, slab_sems2.at[1, u])
+                    there = TILES[u][1]
 
             def unpack(s, carry, half=half):
                 rows = []
                 for eight in range(2):
-                    held = got_slab[2 * p + half, pl.ds(4 * s + 2 * eight, 2)].astype(jnp.float32)
+                    held = got_slab[p, pl.ds(4 * s + 2 * eight, 2), pl.ds(2 * half, 2)].astype(jnp.float32)
                     rows.append(jnp.swapaxes(held.reshape(8, 8, 128), 0, 1))
                 at = pl.multiple_of(half * 128 + s * 16, 16)
                 freq_back[:, pl.ds(at, 16), :] = jnp.concatenate(rows, axis=1).astype(BF)
@@ -613,20 +644,20 @@
     spread(1)
     cut(1)
     send_sides(1)
-    x_stage(0)
-    x_stage(1)
+    for u in UNITS_OF[0]:
+        x_stage(u)
     inner_z(1)
     outer_z(1)
-    y_stage(0)
-    y_stage(1)
-    x_stage(2)
-    x_stage(3)
-    i_stage(0)
-    i_stage(1)
-    y_stage(2)
-    y_stage(3)
-    i_stage(2)
-    i_stage(3)
+    for u in UNITS_OF[0]:
+        y_stage(u)
+    for u in UNITS_OF[1]:
+        x_stage(u)
+    for u in UNITS_OF[0]:
+        i_stage(u)
+    for u in UNITS_OF[1]:
+        y_stage(u)
+    for u in UNITS_OF[1]:
+        i_stage(u)
     home(0)
     send_back_rims(0)
     home(1)
@@ -638,10 +669,10 @@
     for copy in near.values():
         copy.wait_send()
     for u in range(UNITS):
-        wait(block, u, SLABS, slab_sems, 0)
-        wait(back_slab, u, SLABS, slab_sems2, 0)
-        wait(to_brick, u, BRICKS, brick_sems, 0)
-        wait(back_brick, u, BRICKS, brick_sems2, 0)
+        wait_slabs(block, u, slab_sems.at[0, u])
+        wait_bricks(to_brick, u, brick_sems.at[0, u])
+        wait_bricks(back_brick, u, brick_sems2.at[0, u])
+        wait_slabs(back_slab, u, slab_sems2.at[0, u])
 
 
 def body(charges, fractions, inner_cell, dest_slab, filter_amp):
@@ -650,8 +681,8 @@
     dma = pltpu.SemaphoreType.DMA
     atoms = charges.shape[1]
     tables = [jnp.asarray(table) for table in make_tables()]
-    to_slab = (UNITS, SLABS, 2, 16, 128)
-    to_brick = (UNITS, BRICKS, 4, 64, 128)
+    to_slab = (2, SLABS, 4, 16, 128)
+    to_brick = (2, BRICKS, 8, 64, 128)
     return pl.pallas_call(
         kernel,
         out_shape=jax.ShapeDtypeStruct((4, atoms), jnp.float32),
@@ -685,7 +716,7 @@
         + [pltpu.VMEM(to_brick, BF)] * 4
         + [pltpu.VMEM(to_slab, BF)] * 2
         + [
-            pltpu.VMEM((512, 512), jnp.float32),
+            pltpu.VMEM((512, 4 * 128), jnp.float32),
             pltpu.VMEM((2, WIDE, G, 128), BF),
             pltpu.VMEM((2, 512, G), jnp.float32),
             dma((len(tables),)),

time: 71.6 us -> 71.7 us (level)
  no operation moved by 1% of the time
where the time goes in v4:
time: 71.7 us; the launch traced here: 71.4 us
  Pallas kernels  70.1 us (98%)
  local copies, waits for them, and re-layouts  1.32 us (2%)
    pallas_call x1, Pallas kernels, body(): pl.pallas_call(kernel, out_shape=jax.ShapeDtypeStruct((4, atoms), jnp.flo...  70.1 us

profile of v4, /device:TPU:0, one launch (start us, length us, event | category | flops | bytes accessed | tf_op | source)
XLA Modules:
  0.0 71.4 jit_solution(8726785854005721959)
XLA Ops:
  0.0 70.1 %shard_map.118 = f32[4,1024]{1,0:T(4,128)} custom-call(f32[4,1024]{1,0:T(4,128)} %charge_ref.1, f32[3,1024]{1,0:T(4,128)} %frac_ref.1, s32[1,1024]{1,0:T(1,128)} %bitcast.2, s32[1,1024]{1,0:T(1,128)} %bitcast.3, f32[2,16]{1,0:T(2,128)} %amp_ref.1, bf16[128,1408]{1,0:T(8,128)(2,1)} %constant.14.clone.rim_far, bf16[512,256]{1,0:T(8,128)(2,1)} %constant.15.clone.zt_far, ...), custom_call_target="tpu_custom_call" | custom-call | tf_op jit(solution)/shard_map/pallas_call | solution.py:686
  70.1 1.3 %copy.14 = f32[4,1024]{1,0:T(4,128)} copy(f32[4,1024]{1,0:T(4,128)} %shard_map.118) | data formatting | bytes 32768

commit v5 on v4

--- a/solution.py
+++ b/solution.py
@@ -642,22 +642,28 @@
     make_gain()
     outer_z(0)
     spread(1)
+    x_stage(0)
     cut(1)
+    x_stage(1)
     send_sides(1)
-    for u in UNITS_OF[0]:
-        x_stage(u)
+    x_stage(2)
     inner_z(1)
+    y_stage(0)
     outer_z(1)
-    for u in UNITS_OF[0]:
-        y_stage(u)
-    for u in UNITS_OF[1]:
-        x_stage(u)
-    for u in UNITS_OF[0]:
-        i_stage(u)
-    for u in UNITS_OF[1]:
-        y_stage(u)
-    for u in UNITS_OF[1]:
-        i_stage(u)
+    y_stage(1)
+    y_stage(2)
+    i_stage(0)
+    x_stage(3)
+    x_stage(4)
+    x_stage(5)
+    i_stage(1)
+    y_stage(3)
+    i_stage(2)
+    y_stage(4)
+    y_stage(5)
+    i_stage(3)
+    i_stage(4)
+    i_stage(5)
     home(0)
     send_back_rims(0)
     home(1)

time: 71.7 us -> 72.8 us (1.015)
  Pallas kernels: 70.1 us -> 71.2 us
    pallas_call x1, Pallas kernels: 70.1 us -> 71.2 us  [body(): pl.pallas_call(kernel, out_shape=jax.ShapeDtypeStruct((4, atoms), jnp.flo...]
where the time goes in v5:
time: 72.8 us; the launch traced here: 72.5 us
  Pallas kernels  71.2 us (98%)
  local copies, waits for them, and re-layouts  1.32 us (2%)
    pallas_call x1, Pallas kernels, body(): pl.pallas_call(kernel, out_shape=jax.ShapeDtypeStruct((4, atoms), jnp.flo...  71.2 us

profile of v5, /device:TPU:0, one launch (start us, length us, event | category | flops | bytes accessed | tf_op | source)
XLA Modules:
  0.0 72.5 jit_solution(5393602988760798646)
XLA Ops:
  0.0 71.2 %shard_map.118 = f32[4,1024]{1,0:T(4,128)} custom-call(f32[4,1024]{1,0:T(4,128)} %charge_ref.1, f32[3,1024]{1,0:T(4,128)} %frac_ref.1, s32[1,1024]{1,0:T(1,128)} %bitcast.2, s32[1,1024]{1,0:T(1,128)} %bitcast.3, f32[2,16]{1,0:T(2,128)} %amp_ref.1, bf16[128,1408]{1,0:T(8,128)(2,1)} %constant.14.clone.rim_far, bf16[512,256]{1,0:T(8,128)(2,1)} %constant.15.clone.zt_far, ...), custom_call_target="tpu_custom_call" | custom-call | tf_op jit(solution)/shard_map/pallas_call | solution.py:692
  71.2 1.3 %copy.14 = f32[4,1024]{1,0:T(4,128)} copy(f32[4,1024]{1,0:T(4,128)} %shard_map.118) | data formatting | bytes 32768

commit v6 on v4

--- a/solution.py
+++ b/solution.py
@@ -656,9 +656,9 @@
         i_stage(u)
     for u in UNITS_OF[1]:
         y_stage(u)
+    home(0)
     for u in UNITS_OF[1]:
         i_stage(u)
-    home(0)
     send_back_rims(0)
     home(1)
     read_mesh(0)

time: 71.7 us -> 71.1 us (level)
  no operation moved by 1% of the time
where the time goes in v6:
time: 71.1 us; the launch traced here: 70.8 us
  Pallas kernels  69.5 us (98%)
  local copies, waits for them, and re-layouts  1.32 us (2%)
    pallas_call x1, Pallas kernels, body(): pl.pallas_call(kernel, out_shape=jax.ShapeDtypeStruct((4, atoms), jnp.flo...  69.5 us

profile of v6, /device:TPU:0, one launch (start us, length us, event | category | flops | bytes accessed | tf_op | source)
XLA Modules:
  0.0 70.8 jit_solution(17735653564585514391)
XLA Ops:
  0.0 69.5 %shard_map.118 = f32[4,1024]{1,0:T(4,128)} custom-call(f32[4,1024]{1,0:T(4,128)} %charge_ref.1, f32[3,1024]{1,0:T(4,128)} %frac_ref.1, s32[1,1024]{1,0:T(1,128)} %bitcast.2, s32[1,1024]{1,0:T(1,128)} %bitcast.3, f32[2,16]{1,0:T(2,128)} %amp_ref.1, bf16[128,1408]{1,0:T(8,128)(2,1)} %constant.14.clone.rim_far, bf16[512,256]{1,0:T(8,128)(2,1)} %constant.15.clone.zt_far, ...), custom_call_target="tpu_custom_call" | custom-call | tf_op jit(solution)/shard_map/pallas_call | solution.py:686
  69.5 1.3 %copy.14 = f32[4,1024]{1,0:T(4,128)} copy(f32[4,1024]{1,0:T(4,128)} %shard_map.118) | data formatting | bytes 32768

commit v7 on v6

--- a/solution.py
+++ b/solution.py
@@ -616,6 +616,7 @@
 
         lax.fori_loop(0, GROUPS, one, 0, unroll=8)
 
+    def to_atoms(p):
         def unsort(g, total):
             rows = []
             for part in double(read_ref[:, pl.ds(pl.multiple_of(g * 512, 512), 512)]):
@@ -660,12 +661,14 @@
     for u in UNITS_OF[1]:
         i_stage(u)
     send_back_rims(0)
+    read_mesh(0)
     home(1)
-    read_mesh(0)
+    read_rims(0)
     send_back_rims(1)
-    read_rims(0)
+    to_atoms(0)
     read_mesh(1)
     read_rims(1)
+    to_atoms(1)
     for copy in near.values():
         copy.wait_send()
     for u in range(UNITS):

time: 71.1 us -> 71.1 us (level)
  no operation moved by 1% of the time
where the time goes in v7:
time: 71.1 us; the launch traced here: 70.8 us
  Pallas kernels  69.5 us (98%)
  local copies, waits for them, and re-layouts  1.32 us (2%)
    pallas_call x1, Pallas kernels, body(): pl.pallas_call(kernel, out_shape=jax.ShapeDtypeStruct((4, atoms), jnp.flo...  69.5 us

profile of v7, /device:TPU:0, one launch (start us, length us, event | category | flops | bytes accessed | tf_op | source)
XLA Modules:
  0.0 70.8 jit_solution(15109028515582105597)
XLA Ops:
  0.0 69.5 %shard_map.118 = f32[4,1024]{1,0:T(4,128)} custom-call(f32[4,1024]{1,0:T(4,128)} %charge_ref.1, f32[3,1024]{1,0:T(4,128)} %frac_ref.1, s32[1,1024]{1,0:T(1,128)} %bitcast.2, s32[1,1024]{1,0:T(1,128)} %bitcast.3, f32[2,16]{1,0:T(2,128)} %amp_ref.1, bf16[128,1408]{1,0:T(8,128)(2,1)} %constant.14.clone.rim_far, bf16[512,256]{1,0:T(8,128)(2,1)} %constant.15.clone.zt_far, ...), custom_call_target="tpu_custom_call" | custom-call | tf_op jit(solution)/shard_map/pallas_call | solution.py:689
  69.5 1.3 %copy.14 = f32[4,1024]{1,0:T(4,128)} copy(f32[4,1024]{1,0:T(4,128)} %shard_map.118) | data formatting | bytes 32768
